TPU v7x, 32 devices: a whole 2x2x4 slice. The times are simulated.
32 devices in a mesh: pipe: 2 (over core), dp: 16 (over z, y, x).
Axes of the slice: x: 2, y: 2, z: 4, core: 2. Of those that a mesh axis runs over, the one named last changes fastest.
Arguments:
- inputs: bfloat16 [2, 32, 512, 512], P('pipe', 'dp'), may hold values from -6 to 6
- src_len: int32 [32], P('dp'), may hold values from 128 to 512, as said below
- tgt_len: int32 [32], P('dp'), may hold values from 128 to 512, as said below
- groups: int32 [32], P('dp'), may hold values from 0 to 7
- cotangent: bfloat16 [2, 32, 512, 512], P('pipe', 'dp'), may hold values from -6 to 6
- attn_w: bfloat16 [2, 512, 2048], P('pipe'), as said below
- ffn_in: bfloat16 [2, 512, 2048], P('pipe'), may hold values from -0.25 to 0.25
- ffn_in_bias: bfloat16 [2, 2048], P('pipe'), may hold values from -3 to 3
- ffn_out: bfloat16 [2, 2048, 512], P('pipe'), may hold values from -0.125 to 0.125
- ffn_out_bias: bfloat16 [2, 512], P('pipe'), may hold values from -2 to 2
- norm_gain: bfloat16 [2, 2, 512], P('pipe'), may hold values from 0.5 to 1.5
- norm_bias: bfloat16 [2, 2, 512], P('pipe'), may hold values from -2 to 2
- cross_w: bfloat16 [512, 2048], P(None, 'pipe'), as said below
- cross_gain: bfloat16 [512], replicated, may hold values from 0.5 to 1.5
- cross_bias: bfloat16 [512], replicated, may hold values from -2 to 2
- pair_table: bfloat16 [8, 512], replicated, may hold values from -3 to 3
Outputs:
- outputs: float32 [2, 32, 512, 512], P('pipe', 'dp')
- input_grads: float32 [2, 32, 512, 512], P('pipe', 'dp')
- attn_w_grad: float32 [2, 512, 2048], P('pipe')
- ffn_in_grad: float32 [2, 512, 2048], P('pipe')
- ffn_in_bias_grad: float32 [2, 2048], P('pipe')
- ffn_out_grad: float32 [2, 2048, 512], P('pipe')
- ffn_out_bias_grad: float32 [2, 512], P('pipe')
- norm_gain_grad: float32 [2, 2, 512], P('pipe')
- norm_bias_grad: float32 [2, 2, 512], P('pipe')
- cross_w_grad: float32 [512, 2048], P(None, 'pipe')
- cross_gain_grad: float32 [512], replicated
- cross_bias_grad: float32 [512], replicated
- pair_table_grad: float32 [8, 512], replicated
Inputs may be any that keep to these rules, and one draw needn't show every extreme that they name: `src_len`: each source length is a whole number; in every draw one pair has exactly 512 and one exactly a quarter of 512 live source positions. `tgt_len`: likewise for target lengths. `attn_w`: independent normal entries; in each section's block the last 512 columns have deviation 0.5, the others deviation 1 / sqrt(512). `cross_w`: independent normal entries; the last 512 columns have deviation 0.5, the others deviation 1 / sqrt(512).
All inputs are finite; a program needn't handle non-finite values.
Results may differ from a plain program's by a relative error of at most 0.013.
Values may be sent and summed in bfloat16 or wider, within the bound.
A program may use at most 256 MiB of HBM per device.

v0:
```python
import jax
import jax.numpy as jnp
from jax import lax
from jax.sharding import PartitionSpec as P

HEADS = 8
BLOCK = 512


norm_epsilon = 1e-05
masked_score = -1e30


def shifted_2(shard, axis, by):
    count = lax.axis_size(axis)
    pairs = [(i, i + by) for i in range(count) if 0 <= i + by < count]
    return lax.ppermute(shard, axis, pairs)


def product(left, right):
    return jnp.dot(left, right, preferred_element_type=jnp.float32)


def product_left(left, right):
    return lax.dot_general(
        left, right, (((0,), (0,)), ((), ())), preferred_element_type=jnp.float32
    )


def product_right(left, right):
    return lax.dot_general(
        left, right, (((1,), (1,)), ((), ())), preferred_element_type=jnp.float32
    )


def gelu_exact(values):
    return 0.5 * values * (1.0 + jax.scipy.special.erf(values * 0.7071067811865476))


def gelu_slope(values):
    cumulative = 0.5 * (1.0 + jax.scipy.special.erf(values * 0.7071067811865476))
    density = jnp.exp(-0.5 * values * values) * 0.3989422804014327
    return cumulative + values * density


def norm_forward(values, gain_row, shift_row):
    centred = values - jnp.mean(values, axis=-1, keepdims=True)
    inverse = lax.rsqrt(jnp.mean(centred * centred, axis=-1, keepdims=True) + norm_epsilon)
    normed = centred * inverse
    return (normed * gain_row + shift_row, (normed, inverse))


def norm_backward(grad_out, saved_norm, gain_row):
    normed, inverse = saved_norm
    grad_normed = grad_out * gain_row
    grad_in = inverse * (
        grad_normed
        - jnp.mean(grad_normed, axis=-1, keepdims=True)
        - normed * jnp.mean(grad_normed * normed, axis=-1, keepdims=True)
    )
    return (grad_in, jnp.sum(grad_out * normed, axis=0), jnp.sum(grad_out, axis=0))


def allowed_keys(key_live, first_row, block_rows, causal):
    allowed = jnp.broadcast_to(key_live[None, :] > 0.5, (block_rows, key_live.shape[0]))
    if causal:
        query_index = first_row + jnp.arange(block_rows, dtype=jnp.int32)
        key_index = jnp.arange(key_live.shape[0], dtype=jnp.int32)
        allowed = allowed & (key_index[None, :] <= query_index[:, None])
    return allowed


def attend_forward(queries, key_rows, value_rows, key_live, causal):
    row_count, features = queries.shape
    head_dim = features // HEADS
    block_rows = min(BLOCK, row_count)
    block_count = row_count // block_rows
    score_scale = head_dim ** (-0.5)
    key_heads = key_rows.reshape(-1, HEADS, head_dim)
    value_heads = value_rows.reshape(-1, HEADS, head_dim)

    def one_block(block_index):
        first_row = block_index * block_rows
        query_heads = queries.reshape(block_rows, HEADS, head_dim)
        scores = (
            jnp.einsum("qhd,khd->hqk", query_heads, key_heads, preferred_element_type=jnp.float32)
            * score_scale
        )
        allowed = allowed_keys(key_live, first_row, block_rows, causal)
        scores = jnp.where(allowed[None], scores, masked_score)
        row_max = jnp.max(scores, axis=-1, keepdims=True)
        shifted = jnp.exp(scores - row_max)
        row_total = jnp.sum(shifted, axis=-1, keepdims=True)
        soft_weights = (shifted / row_total).astype(jnp.bfloat16)
        mixed_rows = jnp.einsum(
            "hqk,khd->qhd", soft_weights, value_heads, preferred_element_type=jnp.float32
        )
        return (
            mixed_rows.reshape(block_rows, features).astype(jnp.bfloat16),
            (row_max + jnp.log(row_total))[..., 0],
        )

    mixed_blocks, log_totals = lax.map(one_block, jnp.arange(block_count, dtype=jnp.int32))
    return (mixed_blocks.reshape(row_count, features), log_totals)


def attend_backward(queries, key_rows, value_rows, key_live, causal, log_totals, grad_mixed):
    row_count, features = queries.shape
    head_dim = features // HEADS
    block_rows = min(BLOCK, row_count)
    block_count = row_count // block_rows
    score_scale = head_dim ** (-0.5)
    key_heads = key_rows.reshape(-1, HEADS, head_dim)
    value_heads = value_rows.reshape(-1, HEADS, head_dim)

    def one_block(carry, block_index):
        grad_keys, grad_values = carry
        first_row = block_index * block_rows
        query_heads = queries.reshape(block_rows, HEADS, head_dim)
        grad_heads = grad_mixed.reshape(block_rows, HEADS, head_dim)
        scores = (
            jnp.einsum("qhd,khd->hqk", query_heads, key_heads, preferred_element_type=jnp.float32)
            * score_scale
        )
        allowed = allowed_keys(key_live, first_row, block_rows, causal)
        block_totals = lax.dynamic_index_in_dim(log_totals, block_index, 0, keepdims=False)
        soft_weights = jnp.where(allowed[None], jnp.exp(scores - block_totals[..., None]), 0.0)
        grad_values = grad_values + jnp.einsum(
            "hqk,qhd->khd",
            soft_weights.astype(jnp.bfloat16),
            grad_heads,
            preferred_element_type=jnp.float32,
        )
        grad_weights = jnp.einsum(
            "qhd,khd->hqk", grad_heads, value_heads, preferred_element_type=jnp.float32
        )
        centre = jnp.sum(soft_weights * grad_weights, axis=-1, keepdims=True)
        grad_scores = (soft_weights * (grad_weights - centre)).astype(jnp.bfloat16)
        grad_query = (
            jnp.einsum("hqk,khd->qhd", grad_scores, key_heads, preferred_element_type=jnp.float32)
            * score_scale
        )
        grad_keys = (
            grad_keys
            + jnp.einsum(
                "hqk,qhd->khd", grad_scores, query_heads, preferred_element_type=jnp.float32
            )
            * score_scale
        )
        return ((grad_keys, grad_values), grad_query.reshape(block_rows, features))

    zero_heads = jnp.zeros(key_heads.shape, jnp.float32)
    (grad_keys, grad_values), grad_blocks = lax.scan(
        one_block, (zero_heads, zero_heads), jnp.arange(block_count, dtype=jnp.int32)
    )
    return (
        grad_blocks.reshape(row_count, features),
        grad_keys.reshape(-1, features),
        grad_values.reshape(-1, features),
    )


def attention_forward(rows_round, attn_block, key_live, causal):
    features = rows_round.shape[1]
    packed = product(rows_round, attn_block[:, : 3 * features]).astype(jnp.bfloat16)
    mixed_rows, log_totals = attend_forward(
        packed[:, :features],
        packed[:, features : 2 * features],
        packed[:, 2 * features :],
        key_live,
        causal,
    )
    added = product(mixed_rows, attn_block[:, 3 * features :])
    return (added, (packed, mixed_rows, log_totals))


def attention_backward(grad_added, rows_round, attn_block, key_live, causal, kept_attn):
    packed, mixed_rows, log_totals = kept_attn
    features = rows_round.shape[1]
    grad_round = grad_added.astype(jnp.bfloat16)
    grad_out_weight = product_left(mixed_rows, grad_round)
    grad_mixed = product_right(grad_round, attn_block[:, 3 * features :]).astype(jnp.bfloat16)
    grad_query, grad_keys, grad_values = attend_backward(
        packed[:, :features],
        packed[:, features : 2 * features],
        packed[:, 2 * features :],
        key_live,
        causal,
        log_totals,
        grad_mixed,
    )
    grad_packed = jnp.concatenate([grad_query, grad_keys, grad_values], axis=1).astype(jnp.bfloat16)
    grad_in_weight = product_left(rows_round, grad_packed)
    grad_rows = product_right(grad_packed, attn_block[:, : 3 * features])
    return (grad_rows, jnp.concatenate([grad_in_weight, grad_out_weight], axis=1))


def ffn_forward(hidden_round, ffn_first, bias_first, ffn_second, bias_second):
    inner = product(hidden_round, ffn_first) + bias_first
    active = gelu_exact(inner).astype(jnp.bfloat16)
    return (product(active, ffn_second) + bias_second, (inner, active))


def ffn_backward(grad_branch, hidden_round, ffn_first, ffn_second, kept_ffn):
    inner, active = kept_ffn
    grad_round = grad_branch.astype(jnp.bfloat16)
    grad_second = product_left(active, grad_round)
    grad_bias_second = jnp.sum(grad_round.astype(jnp.float32), axis=0)
    grad_inner = (product_right(grad_round, ffn_second) * gelu_slope(inner)).astype(jnp.bfloat16)
    grad_first = product_left(hidden_round, grad_inner)
    grad_bias_first = jnp.sum(grad_inner.astype(jnp.float32), axis=0)
    grad_hidden = product_right(grad_inner, ffn_first)
    return (grad_hidden, (grad_first, grad_bias_first, grad_second, grad_bias_second))


def source_rows(source, tag_row):
    residual = source.astype(jnp.float32) + tag_row[None, :]
    return (residual, residual.astype(jnp.bfloat16))


def encoder_forward(source, tag_row, source_live, section):
    attn_block, ffn_first, bias_first, ffn_second, bias_second, gains, shifts, cross_block = section
    residual, rows_round = source_rows(source, tag_row)
    added, kept_attn = attention_forward(rows_round, attn_block, source_live, False)
    first_norm, saved_first = norm_forward(residual + added, gains[0], shifts[0])
    hidden_round = first_norm.astype(jnp.bfloat16)
    branch, kept_ffn = ffn_forward(hidden_round, ffn_first, bias_first, ffn_second, bias_second)
    final, saved_final = norm_forward(residual + first_norm + branch, gains[1], shifts[1])
    memory = final * source_live[:, None]
    memory_round = memory.astype(jnp.bfloat16)
    memory_kv = product(memory_round, cross_block).astype(jnp.bfloat16)
    kept = (kept_attn, saved_first, hidden_round, kept_ffn, saved_final, memory_round)
    return (memory, memory_kv, kept)


def encoder_backward(
    source, tag_row, hot_row, source_live, section, kept, grad_memory, grad_kv, shared_like
):
    attn_block, ffn_first, bias_first, ffn_second, bias_second, gains, shifts, cross_block = section
    kept_attn, saved_first, hidden_round, kept_ffn, saved_final, memory_round = kept
    rows_round = source_rows(source, tag_row)[1]
    grad_cross = product_left(memory_round, grad_kv)
    grad_total = (grad_memory + product_right(grad_kv, cross_block)) * source_live[:, None]
    grad_sum, grad_gain_last, grad_shift_last = norm_backward(grad_total, saved_final, gains[1])
    grad_hidden, ffn_grads = ffn_backward(grad_sum, hidden_round, ffn_first, ffn_second, kept_ffn)
    grad_first, grad_gain_first, grad_shift_first = norm_backward(
        grad_sum + grad_hidden, saved_first, gains[0]
    )
    grad_rows, grad_attn = attention_backward(
        grad_first, rows_round, attn_block, source_live, False, kept_attn
    )
    grad_source = grad_sum + grad_first + grad_rows
    grad_pairs = hot_row[:, None] * jnp.sum(grad_source, axis=0)[None, :]
    grads = (
        grad_attn,
        ffn_grads[0],
        ffn_grads[1],
        ffn_grads[2],
        ffn_grads[3],
        jnp.stack([grad_gain_first, grad_gain_last]),
        jnp.stack([grad_shift_first, grad_shift_last]),
        grad_cross,
        jnp.zeros(shared_like[0].shape, jnp.float32),
        jnp.zeros(shared_like[1].shape, jnp.float32),
        grad_pairs,
    )
    return (grad_source, grads)


def decoder_step(
    target, tag_row, target_live, source_live, memory_kv, grad_output, section, cross_norm, hot_row
):
    attn_block, ffn_first, bias_first, ffn_second, bias_second, gains, shifts, cross_block = section
    cross_gain, cross_bias = cross_norm
    features = target.shape[1]
    residual = target.astype(jnp.float32) + tag_row[None, :]
    rows_round = residual.astype(jnp.bfloat16)
    added, kept_attn = attention_forward(rows_round, attn_block, target_live, True)
    first_norm, saved_first = norm_forward(residual + added, gains[0], shifts[0])
    first_round = first_norm.astype(jnp.bfloat16)
    cross_query = product(first_round, cross_block[:, :features]).astype(jnp.bfloat16)
    cross_mixed, cross_totals = attend_forward(
        cross_query, memory_kv[:, :features], memory_kv[:, features:], source_live, False
    )
    cross_added = product(cross_mixed, cross_block[:, features:])
    second_norm, saved_second = norm_forward(first_norm + cross_added, cross_gain, cross_bias)
    second_round = second_norm.astype(jnp.bfloat16)
    branch, kept_ffn = ffn_forward(second_round, ffn_first, bias_first, ffn_second, bias_second)
    final, saved_final = norm_forward(residual + second_norm + branch, gains[1], shifts[1])
    decoded = final * target_live[:, None]
    grad_total = grad_output.astype(jnp.float32) * target_live[:, None]
    grad_sum, grad_gain_last, grad_shift_last = norm_backward(grad_total, saved_final, gains[1])
    grad_hidden, ffn_grads = ffn_backward(grad_sum, second_round, ffn_first, ffn_second, kept_ffn)
    grad_second, grad_cross_gain, grad_cross_bias = norm_backward(
        grad_sum + grad_hidden, saved_second, cross_gain
    )
    cross_round = grad_second.astype(jnp.bfloat16)
    grad_cross_out = product_left(cross_mixed, cross_round)
    grad_cross_mixed = product_right(cross_round, cross_block[:, features:]).astype(jnp.bfloat16)
    grad_cquery, grad_ckeys, grad_cvalues = attend_backward(
        cross_query,
        memory_kv[:, :features],
        memory_kv[:, features:],
        source_live,
        False,
        cross_totals,
        grad_cross_mixed,
    )
    query_round = grad_cquery.astype(jnp.bfloat16)
    grad_cross_query = product_left(first_round, query_round)
    grad_kv = jnp.concatenate([grad_ckeys, grad_cvalues], axis=1).astype(jnp.bfloat16)
    grad_first_in = grad_second + product_right(query_round, cross_block[:, :features])
    grad_first, grad_gain_first, grad_shift_first = norm_backward(
        grad_first_in, saved_first, gains[0]
    )
    grad_rows, grad_attn = attention_backward(
        grad_first, rows_round, attn_block, target_live, True, kept_attn
    )
    grad_target = grad_sum + grad_first + grad_rows
    grad_pairs = hot_row[:, None] * jnp.sum(grad_target, axis=0)[None, :]
    grads = (
        grad_attn,
        ffn_grads[0],
        ffn_grads[1],
        ffn_grads[2],
        ffn_grads[3],
        jnp.stack([grad_gain_first, grad_gain_last]),
        jnp.stack([grad_shift_first, grad_shift_last]),
        jnp.concatenate([grad_cross_query, grad_cross_out], axis=1),
        grad_cross_gain,
        grad_cross_bias,
        grad_pairs,
    )
    return (decoded, grad_target, grad_kv, grads)


def either(flag, work, operands):

    def nothing(inner_operands):
        return jax.tree.map(jnp.zeros_like, work(inner_operands))

    return lax.cond(flag, work, nothing, operands)


def body(
    inputs,
    src_len,
    tgt_len,
    groups,
    cotangent,
    attn_w,
    ffn_in,
    ffn_in_bias,
    ffn_out,
    ffn_out_bias,
    norm_gain,
    norm_bias,
    cross_w,
    cross_gain,
    cross_bias,
    pair_table,
):
    micro = inputs.shape[1]
    seq_rows = inputs.shape[2]
    first_section = lax.axis_index("pipe") == 0
    later_section = jnp.logical_not(first_section)
    section = (
        attn_w[0],
        ffn_in[0],
        ffn_in_bias[0].astype(jnp.float32),
        ffn_out[0],
        ffn_out_bias[0].astype(jnp.float32),
        norm_gain[0].astype(jnp.float32),
        norm_bias[0].astype(jnp.float32),
        cross_w,
    )
    cross_norm = (cross_gain.astype(jnp.float32), cross_bias.astype(jnp.float32))
    shared_like = (cross_gain, cross_bias, pair_table)
    positions = jnp.arange(seq_rows, dtype=jnp.int32)
    source_live = (positions[None, :] < src_len[:, None]).astype(jnp.float32)
    target_live = (positions[None, :] < tgt_len[:, None]).astype(jnp.float32)
    pair_hot = (
        groups[:, None] == jnp.arange(pair_table.shape[0], dtype=jnp.int32)[None, :]
    ).astype(jnp.float32)
    tag_rows = product(pair_hot.astype(jnp.bfloat16), pair_table)
    grads = tuple(
        (
            jnp.zeros(member.shape, jnp.float32)
            for member in (
                attn_w[0],
                ffn_in[0],
                ffn_in_bias[0],
                ffn_out[0],
                ffn_out_bias[0],
                norm_gain[0],
                norm_bias[0],
                cross_w,
                cross_gain,
                cross_bias,
                pair_table,
            )
        )
    )

    def encoder_work(operands):
        source_row, tag_row, live_row = operands
        memory, memory_kv, kept = encoder_forward(source_row, tag_row, live_row, section)
        return (memory, memory_kv, kept)

    def encoder_back(operands):
        source_row, tag_row, hot_row, live_row, grad_row, grad_kv, kept = operands
        return encoder_backward(
            source_row,
            tag_row,
            hot_row,
            live_row,
            section,
            kept,
            grad_row.astype(jnp.float32),
            grad_kv,
            shared_like,
        )

    def decoder_work(operands):
        target_row, tag_row, live_row, source_row_live, memory_kv, grad_row, hot_row = operands
        return decoder_step(
            target_row,
            tag_row,
            live_row,
            source_row_live,
            memory_kv,
            grad_row,
            section,
            cross_norm,
            hot_row,
        )

    outputs = jnp.zeros((micro, seq_rows, inputs.shape[3]), jnp.float32)
    input_grads = jnp.zeros_like(outputs)
    arrived_kv = [None] * micro
    arrived_grad = [None] * micro
    kept_store = [None] * micro
    for step_index in range(micro + 2):
        back_slot = step_index - 2
        if back_slot >= 0:
            grad_source, extra = either(
                first_section,
                encoder_back,
                (
                    inputs[0, back_slot],
                    tag_rows[back_slot],
                    pair_hot[back_slot],
                    source_live[back_slot],
                    cotangent[0, back_slot],
                    arrived_grad[back_slot],
                    kept_store[back_slot],
                ),
            )
            input_grads = input_grads.at[back_slot].add(grad_source)
            grads = jax.tree.map(jnp.add, grads, extra)
        decoder_slot = step_index - 1
        if 0 <= decoder_slot < micro:
            decoded, grad_target, grad_kv, extra = either(
                later_section,
                decoder_work,
                (
                    inputs[0, decoder_slot],
                    tag_rows[decoder_slot],
                    target_live[decoder_slot],
                    source_live[decoder_slot],
                    arrived_kv[decoder_slot],
                    cotangent[0, decoder_slot],
                    pair_hot[decoder_slot],
                ),
            )
            outputs = outputs.at[decoder_slot].add(decoded)
            input_grads = input_grads.at[decoder_slot].add(grad_target)
            grads = jax.tree.map(jnp.add, grads, extra)
            arrived_grad[decoder_slot] = shifted_2(grad_kv, "pipe", -1)
        if step_index < micro:
            memory, memory_kv, kept = either(
                first_section,
                encoder_work,
                (inputs[0, step_index], tag_rows[step_index], source_live[step_index]),
            )
            outputs = outputs.at[step_index].add(memory)
            kept_store[step_index] = kept
            arrived_kv[step_index] = shifted_2(memory_kv, "pipe", 1)
    summed_section = lax.psum(
        (grads[0], grads[1], grads[2], grads[3], grads[4], grads[5], grads[6], grads[7]), "dp"
    )
    summed_shared = lax.psum((grads[8], grads[9], grads[10]), ("pipe", "dp"))
    summed = tuple(summed_section) + tuple(summed_shared)
    return (
        outputs[None],
        input_grads[None],
        summed[0][None],
        summed[1][None],
        summed[2][None],
        summed[3][None],
        summed[4][None],
        summed[5][None],
        summed[6][None],
        summed[7],
        summed[8],
        summed[9],
        summed[10],
    )


def solution(mesh):
    return jax.shard_map(
        body,
        mesh=mesh,
        in_specs=(
            P("pipe", "dp", None, None),
            P("dp"),
            P("dp"),
            P("dp"),
            P("pipe", "dp", None, None),
            P("pipe", None, None),
            P("pipe", None, None),
            P("pipe", None),
            P("pipe", None, None),
            P("pipe", None),
            P("pipe", None, None),
            P("pipe", None, None),
            P(None, "pipe"),
            P(),
            P(),
            P(),
        ),
        out_specs=(
            P("pipe", "dp", None, None),
            P("pipe", "dp", None, None),
            P("pipe", None, None),
            P("pipe", None, None),
            P("pipe", None),
            P("pipe", None, None),
            P("pipe", None),
            P("pipe", None, None),
            P("pipe", None, None),
            P(None, "pipe"),
            P(),
            P(),
            P(),
        ),
        check_vma=False,
    )
```

profile of v0, /device:TPU:0, one launch (start us, length us, event | category | flops | bytes accessed | tf_op | source)
XLA Modules:
  0.0 773.6 jit_solution(14061728562043589578)
XLA Ops:
  13.0 33.7 %conditional.6 = (bf16[512,1024]{1,0:T(8,128)(2,1)}, bf16[512,1536]{1,0:T(8,128)(2,1)S(1)}, bf16[512,512]{0,1:T(8,128)(2,1)}, f32[1,8,512]{2,1,0:T(8,128)S(1)}, ...) conditional(s32[]{:T(128)} %convert_element_type.462, ...), branch_computations={%region_0.0_spmd, %region_1.8_spmd} | conditional | flops 4337169920 | bytes 110858624 | solution.py:342
  14.0 2.5 convolution_convert_fusion
  22.4 3.1 fusion.5
  28.9 4.8 multiply_convert_fusion
  33.7 3.3 fusion.254
  37.8 2.3 fusion.8
  42.4 2.8 convolution_convert_fusion.1
  46.8 3.0 copy.177
  52.1 36.0 %conditional.8 = (bf16[512,1024]{1,0:T(8,128)(2,1)}, bf16[512,1536]{1,0:T(8,128)(2,1)S(1)}, bf16[512,512]{0,1:T(8,128)(2,1)}, f32[1,8,512]{2,1,0:T(8,128)S(1)}, ...) conditional(s32[]{:T(128)} %convert_element_type.462, ...), branch_computations={%region_37.38_spmd, %region_38.45_spmd} | conditional | flops 4337169920 | bytes 110858608 | solution.py:342
  54.4 2.5 convolution_convert_fusion.6
  62.7 3.0 fusion.97
  69.2 4.8 multiply_convert_fusion.4
  74.0 3.3 fusion.267
  78.1 2.3 fusion.100
  82.7 2.7 convolution_convert_fusion.7
  85.5 2.6 copy.262
  88.1 2.8 copy.184
  90.9 2.7 collective-permute-start.1
  96.6 21.6 %conditional.7 = (bf16[512,1024]{0,1:T(8,128)(2,1)}, f32[512,2048]{1,0:T(8,128)}, f32[512,2048]{1,0:T(8,128)}, f32[2048]{0:T(1024)S(1)}, f32[2048,512]{1,0:T(8,1...) conditional(s32[]{:T(128)} %convert_element_type.474, ...), branch_computations={%region_8.9_spmd, %region_9.37_spmd} | conditional | flops 14675331072 | bytes 546904320 | solution.py:342
  96.6 2.5 broadcast.940
  99.2 2.5 broadcast.940.clone
  101.7 2.5 broadcast.942
  118.3 2.6 copy.189
  122.3 22.8 %conditional.9 = (bf16[512,1024]{0,1:T(8,128)(2,1)}, f32[512,2048]{1,0:T(8,128)}, f32[512,2048]{1,0:T(8,128)}, f32[2048]{0:T(1024)S(1)}, f32[2048,512]{1,0:T(8,1...) conditional(s32[]{:T(128)} %convert_element_type.474, ...), branch_computations={%region_45.46_spmd, %region_46.74_spmd} | conditional | flops 14679525376 | bytes 546892096 | solution.py:342
  123.4 2.4 broadcast.976
  125.8 2.5 broadcast.976.clone
  128.3 2.5 broadcast.978
  145.2 2.6 copy.198
  149.2 67.7 %conditional.10 = (f32[512,2048]{1,0:T(8,128)}, f32[2048]{0:T(1024)S(1)}, f32[512]{0:T(512)S(1)}, f32[2,512]{1,0:T(2,128)S(1)}, f32[2,512]{1,0:T(2,128)S(1)}, /*...) conditional(s32[]{:T(128)} %convert_element_type.462, ...), branch_computations={%region_74.75_spmd.clone, %region_75.88_spmd.clone} | conditional | flops 8923117568 | bytes 241380096 | solution.py:342
  150.9 3.0 copy.191
  153.9 3.1 multiply_reduce_fusion.31
  158.1 5.1 convert_reduce_fusion.4
  166.5 2.9 convolution_bitcast_fusion.2
  178.1 2.9 multiply_reduce_fusion.30
  180.9 3.0 multiply_convert_fusion.8
  187.4 2.4 pad_maximum_fusion.16
  189.9 3.8 fusion.286
  195.8 4.9 convolution_bitcast_fusion.1
  200.7 5.4 copy.270
  206.2 5.0 convolution_bitcast_fusion
  211.1 5.4 copy.272
  216.9 18.4 %collective-permute-done.3 = bf16[512,1024]{1,0:T(8,128)(2,1)} collective-permute-done((bf16[512,1024]{1,0:T(8,128)(2,1)}, bf16[512,1024]{1,0:T(8,128)(2,1)}, u32[]{:S(2)}, u32[]{:S(2)}) %collective-permute-start.3) | collective-permute-done | bytes 1048608 | tf_op jit(solution)/shard_map/ppermute | solution.py:17
  235.3 65.5 %conditional.11 = (f32[512,2048]{1,0:T(8,128)}, f32[2048]{0:T(1024)S(1)}, f32[512]{0:T(512)S(1)}, f32[2,512]{1,0:T(2,128)S(1)}, f32[2,512]{1,0:T(2,128)S(1)}, /*...) conditional(s32[]{:T(128)} %convert_element_type.462, ...), branch_computations={%region_88.89_spmd.clone, %region_89.102_spmd.clone} | conditional | flops 8923117568 | bytes 224594368 | solution.py:342
  237.0 2.9 copy.200
  239.9 3.1 multiply_reduce_fusion.38
  244.1 5.1 convert_reduce_fusion.6
  252.4 2.5 convolution_bitcast_fusion.5
  262.7 2.9 multiply_reduce_fusion.37
  265.6 3.0 multiply_convert_fusion.9
  272.0 2.4 pad_maximum_fusion.22
  274.5 3.5 fusion.288
  280.0 4.9 convolution_bitcast_fusion.4
  284.9 5.5 copy.274
  290.4 4.9 convolution_bitcast_fusion.3
  295.3 5.4 copy.276
  300.8 10.2 %add_bitcast_fusion.4 = f32[1,512,2048]{2,1,0:T(8,128)} fusion(f32[512,2048]{1,0:T(8,128)} %get-tuple-element.1100, f32[512,2048]{1,0:T(8,128)} %get-tuple-element.1048, f32[512,2048]{1,0:T(8,128)} %get-tuple-element.1046, f32[512,2048]{1,0:T(8,128)} %get-tuple-element.1088), kind=kLoop, calls=%fused_computation.472 | loop fusion | flops 3145728 | bytes 20971520 | tf_op jit(solution)/shard_map/broadcast_in_dim | solution.py:497
  311.0 10.2 %add_bitcast_fusion.3 = f32[1,512,2048]{2,1,0:T(8,128)} fusion(f32[512,2048]{1,0:T(8,128)} %get-tuple-element.1454, f32[512,2048]{1,0:T(8,128)} %get-tuple-element.1052, f32[512,2048]{1,0:T(8,128)} %get-tuple-element.1050, f32[512,2048]{1,0:T(8,128)} %get-tuple-element.1452), kind=kLoop, calls=%fused_computation.471 | loop fusion | flops 3145728 | bytes 20971520 | tf_op jit(solution)/shard_map/broadcast_in_dim | solution.py:498
  321.2 10.0 %add_bitcast_fusion.2 = f32[1,2048,512]{2,1,0:T(8,128)} fusion(f32[2048,512]{1,0:T(8,128)} %get-tuple-element.1455, f32[2048,512]{1,0:T(8,128)} %get-tuple-element.1060, f32[2048,512]{1,0:T(8,128)} %get-tuple-element.1058, f32[2048,512]{1,0:T(8,128)} %get-tuple-element.1453), kind=kLoop, calls=%fused_computation.470 | loop fusion | flops 3145728 | bytes 20971520 | tf_op jit(solution)/shard_map/broadcast_in_dim | solution.py:500
  331.1 5.9 add_add_fusion
  347.6 47.1 %all-reduce.2 = (f32[512]{0:T(512)}, f32[512]{0:T(512)}, f32[8,512]{1,0:T(8,128)}) all-reduce(f32[512]{0:T(512)S(1)} %add_add_fusion.4, f32[512]{0:T(512)S(1)} %add_add_fusion.3, f32[8,512]{1,0:T(8,128)S(1)} %add_add_fusion.1), channel_id=1, replica_groups=mesh['pipe'=2,'dp'=16] {'pipe','dp'}, use_global_device_ids=true, to_apply=%region_110.111 | all-reduce | flops 5120 | bytes 40960 | tf_op jit(solution)/shard_map/psum | solution.py:492
  394.8 78.9 %all-reduce.3 = (f32[1,2048]{1,0:T(1,128)}, f32[1,512]{1,0:T(1,128)}, f32[1,2,512]{2,1,0:T(2,128)}, f32[1,2,512]{2,1,0:T(2,128)}) all-reduce(f32[1,2048]{1,0:T(1,128)S(1)} %bitcast.476, f32[1,512]{1,0:T(1,128)S(1)} %bitcast.529, f32[1,2,512]{2,1,0:T(2,128)S(1)} %add_bitcast_fusion.6, ...), channel_id=1, replica_groups=mesh['pipe'=2,'dp'=16] {'dp'}, use_global_device_ids=true, to_apply=%region_104.105 | all-reduce | flops 4608 | bytes 36864 | tf_op jit(solution)/shard_map/psum | solution.py:489
  474.9 2.6 bitcast_dynamic-update-slice_fusion
  477.5 276.1 %all-reduce.7.cloned.1.call-done = (f32[1,512,2048]{2,1,0:T(8,128)}, f32[1,512,2048]{2,1,0:T(8,128)}, f32[1,2048,512]{2,1,0:T(8,128)}, f32[512,1024]{1,0:T(8,128)}) async-done(((f32[1,512,2048]{2,1,0:T(8,128)}, f32[1,512,2048]{2,1,0:T(8,128)}, f32[1,2048,512]{2,1,0:T(8,128)}, f32[512,1024]{1,0:T(8,128)}), (f32[1,512,2048]{2,1,0:T(8,128)}, f32[1,512,2048]{2,1,0:T(8,128)}, f32[1,2048,512]{2,1,0:T(8,128)}, ...) | async-done | bytes 14680080 | tf_op jit(solution)/shard_map/psum | solution.py:489
  753.6 4.8 copy.467
  (345 shorter events, 112.9 us)
Async XLA Ops:
  7.2 4.3 copy-start
  7.2 746.4 %all-reduce.7.cloned.1.call-start = ((), (), s32[]{:S(2)}) async-start(), calls=%async_computation | async-start | bytes 29360128 | tf_op jit(solution)/shard_map/psum | solution.py:489
  10.7 85.9 %copy-start.147 = (f32[1,2048]{1,0:T(1,128)}, f32[1,2048]{1,0:T(1,128)S(1)}, u32[]{:S(2)}) copy-start(f32[1,2048]{1,0:T(1,128)S(1)} %convert_element_type.502) | copy-start | bytes 24580
  11.4 85.2 %copy-start.158 = (f32[1,512]{1,0:T(1,128)}, f32[1,512]{1,0:T(1,128)S(1)}, u32[]{:S(2)}) copy-start(f32[1,512]{1,0:T(1,128)S(1)} %convert_element_type.503) | copy-start | bytes 6148
  12.3 39.8 %copy-start.162 = (f32[1,512]{1,0:T(1,128)}, f32[1,512]{1,0:T(1,128)S(1)}, u32[]{:S(2)}) copy-start(f32[1,512]{1,0:T(1,128)S(1)} %get-tuple-element.1672) | copy-start | bytes 6148
  12.3 84.3 %copy-start.166 = (f32[1,512]{1,0:T(1,128)}, f32[1,512]{1,0:T(1,128)S(1)}, u32[]{:S(2)}) copy-start(f32[1,512]{1,0:T(1,128)S(1)} %get-tuple-element.1671) | copy-start | bytes 6148
  27.5 6.1 copy-start.125
  28.9 4.8 copy-start.179
  37.0 5.4 copy-start.44
  37.8 8.9 %copy-start.7 = (bf16[512,1536]{1,0:T(8,128)(2,1)S(1)}, bf16[512,1536]{1,0:T(8,128)(2,1)}, u32[]{:S(2)}) copy-start(bf16[512,1536]{1,0:T(8,128)(2,1)} %copy-done.6) | copy-start | bytes 4718596 | tf_op jit(solution)/shard_map/cond
  46.7 5.3 copy-start.18
  46.7 5.3 copy-start.8
  46.8 5.3 copy-start.113
  49.8 46.8 %collective-permute-start = (bf16[512,1024]{0,1:T(8,128)(2,1)}, bf16[512,1024]{0,1:T(8,128)(2,1)}, u32[]{:S(2)}, u32[]{:S(2)}) collective-permute-start(bf16[512,1024]{0,1:T(8,128)(2,1)} %copy.177), channel_id=1, source_target_pairs={{0,16},{1,17},{2,18},{3,19},{4,20},{5,21},{6,22},{7,23},{8,24},{9,... | collective-permute-start | bytes 3145736 | tf_op jit(solution)/shard_map/ppermute | solution.py:17
  52.0 41.5 %copy-start.170 = (bf16[512]{0:T(512)(128)(2,1)S(1)}, bf16[512]{0:T(512)(128)(2,1)}, u32[]{:S(2)}) copy-start(bf16[512]{0:T(512)(128)(2,1)} %param.57) | copy-start | bytes 3076
  52.0 41.5 %copy-start.171 = (bf16[512]{0:T(512)(128)(2,1)S(1)}, bf16[512]{0:T(512)(128)(2,1)}, u32[]{:S(2)}) copy-start(bf16[512]{0:T(512)(128)(2,1)} %param.58) | copy-start | bytes 3076
  52.1 41.5 %copy-start.185 = (s32[2]{0:T(128)S(1)}, s32[2]{0:T(128)}, u32[]{:S(2)}) copy-start(s32[2]{0:T(128)} %param.47) | copy-start | bytes 28
  52.1 42.2 %copy-start.172 = (s32[2]{0:T(128)S(1)}, s32[2]{0:T(128)}, u32[]{:S(2)}) copy-start(s32[2]{0:T(128)} %param.46) | copy-start | bytes 28
  67.8 6.2 copy-start.127
  69.2 4.8 copy-start.180
  77.3 5.4 copy-start.45
  78.1 9.9 %copy-start.11 = (bf16[512,1536]{1,0:T(8,128)(2,1)S(1)}, bf16[512,1536]{1,0:T(8,128)(2,1)}, u32[]{:S(2)}) copy-start(bf16[512,1536]{1,0:T(8,128)(2,1)} %copy-done.10) | copy-start | bytes 4718596 | tf_op jit(solution)/shard_map/cond
  88.0 8.6 %copy-start.12 = (bf16[512,1536]{1,0:T(8,128)(2,1)}, bf16[512,1536]{1,0:T(8,128)(2,1)S(1)}, u32[]{:S(2)}) copy-start(bf16[512,1536]{1,0:T(8,128)(2,1)S(1)} %get-tuple-element.1033) | copy-start | bytes 4718596
  88.0 8.6 %copy-start.115 = (f32[1,8,512]{2,1,0:T(8,128)}, f32[1,8,512]{2,1,0:T(8,128)S(1)}, u32[]{:S(2)}) copy-start(f32[1,8,512]{2,1,0:T(8,128)S(1)} %get-tuple-element.1034) | copy-start | bytes 49156
  88.0 8.5 %copy-start.38 = (bf16[512,512]{1,0:T(8,128)(2,1)S(1)}, bf16[512,512]{1,0:T(8,128)(2,1)}, u32[]{:S(2)}) copy-start(bf16[512,512]{1,0:T(8,128)(2,1)} %copy-done.37) | copy-start | bytes 1572868
  90.9 31.3 %collective-permute-start.1 = (bf16[512,1024]{0,1:T(8,128)(2,1)}, bf16[512,1024]{0,1:T(8,128)(2,1)}, u32[]{:S(2)}, u32[]{:S(2)}) collective-permute-start(bf16[512,1024]{0,1:T(8,128)(2,1)} %copy.184), channel_id=1, source_target_pairs={{0,16},{1,17},{2,18},{3,19},{4,20},{5,21},{6,22},{7,23},{8,24},{9,... | collective-permute-start | bytes 3145736 | tf_op jit(solution)/shard_map/ppermute | solution.py:17
  120.9 28.2 %collective-permute-start.2 = (bf16[512,1024]{1,0:T(8,128)(2,1)}, bf16[512,1024]{1,0:T(8,128)(2,1)}, u32[]{:S(2)}, u32[]{:S(2)}) collective-permute-start(bf16[512,1024]{1,0:T(8,128)(2,1)} %copy.189), channel_id=1, source_target_pairs={{16,0},{17,1},{18,2},{19,3},{20,4},{21,5},{22,6},{23,7},{24,8},{25... | collective-permute-start | bytes 3145736 | tf_op jit(solution)/shard_map/ppermute | solution.py:17
  122.2 26.9 %copy-start.114 = (f32[1,8,512]{2,1,0:T(8,128)S(1)}, f32[1,8,512]{2,1,0:T(8,128)}, u32[]{:S(2)}) copy-start(f32[1,8,512]{2,1,0:T(8,128)} %copy-done.113) | copy-start | bytes 49156
  122.2 26.9 %copy-start.126 = (f32[512,1]{0,1:T(1,128)S(1)}, f32[512,1]{0,1:T(1,128)}, u32[]{:S(2)}) copy-start(f32[512,1]{0,1:T(1,128)} %get-tuple-element.1021) | copy-start | bytes 6148
  145.1 4.0 copy-start.119
  145.2 4.0 copy-start.123
  147.8 87.5 %collective-permute-start.3 = (bf16[512,1024]{1,0:T(8,128)(2,1)}, bf16[512,1024]{1,0:T(8,128)(2,1)}, u32[]{:S(2)}, u32[]{:S(2)}) collective-permute-start(bf16[512,1024]{1,0:T(8,128)(2,1)} %copy.198), channel_id=1, source_target_pairs={{16,0},{17,1},{18,2},{19,3},{20,4},{21,5},{22,6},{23,7},{24,8},{25... | collective-permute-start | bytes 3145736 | tf_op jit(solution)/shard_map/ppermute | solution.py:17
  149.1 86.2 %copy-start.13 = (bf16[512,1536]{1,0:T(8,128)(2,1)S(1)}, bf16[512,1536]{1,0:T(8,128)(2,1)}, u32[]{:S(2)}) copy-start(bf16[512,1536]{1,0:T(8,128)(2,1)} %copy-done.12) | copy-start | bytes 4718596
  149.1 86.2 %copy-start.116 = (f32[1,8,512]{2,1,0:T(8,128)S(1)}, f32[1,8,512]{2,1,0:T(8,128)}, u32[]{:S(2)}) copy-start(f32[1,8,512]{2,1,0:T(8,128)} %copy-done.115) | copy-start | bytes 49156
  149.1 86.2 %copy-start.128 = (f32[512,1]{0,1:T(1,128)S(1)}, f32[512,1]{0,1:T(1,128)}, u32[]{:S(2)}) copy-start(f32[512,1]{0,1:T(1,128)} %get-tuple-element.1035) | copy-start | bytes 6148
  149.2 86.2 %copy-start.154 = (f32[1,8]{1,0:T(1,128)S(1)}, f32[1,8]{1,0:T(1,128)}, u32[]{:S(2)}) copy-start(f32[1,8]{1,0:T(1,128)} %get-tuple-element.1667) | copy-start | bytes 100
  149.2 86.2 %copy-start.163 = (f32[1,512]{1,0:T(1,128)S(1)}, f32[1,512]{1,0:T(1,128)}, u32[]{:S(2)}) copy-start(f32[1,512]{1,0:T(1,128)} %copy-done.162) | copy-start | bytes 6148
  149.2 4.7 copy-start.84
  150.9 12.3 %copy-start.40 = (f32[512,512]{1,0:T(8,128)}, f32[512,512]{1,0:T(8,128)S(1)}, u32[]{:S(2)}) copy-start(f32[512,512]{1,0:T(8,128)S(1)} %copy.192) | copy-start | bytes 3145732 | tf_op jit(solution)/shard_map/cond
  153.9 4.1 copy-start.183
  158.0 5.2 copy-start.52
  158.0 5.2 copy-start.177
  164.8 6.9 copy-start.9
  187.4 6.2 copy-start.15
  187.4 6.2 copy-start.53
  187.4 6.2 copy-start.87
  235.4 4.6 copy-start.82
  237.0 12.2 %copy-start.41 = (f32[512,512]{1,0:T(8,128)}, f32[512,512]{1,0:T(8,128)S(1)}, u32[]{:S(2)}) copy-start(f32[512,512]{1,0:T(8,128)S(1)} %copy.201) | copy-start | bytes 3145732 | tf_op jit(solution)/shard_map/cond
  239.9 4.1 copy-start.184
  244.0 5.2 copy-start.54
  244.0 5.2 copy-start.178
  272.0 5.9 copy-start.55
  272.0 5.9 copy-start.88
  343.9 50.8 %copy-start.141 = (f32[512]{0:T(512)S(1)}, f32[512]{0:T(512)}, u32[]{:S(2)}) copy-start(f32[512]{0:T(512)} %copy-done.140) | copy-start | bytes 6148
  343.9 50.8 %copy-start.144 = (f32[512]{0:T(512)S(1)}, f32[512]{0:T(512)}, u32[]{:S(2)}) copy-start(f32[512]{0:T(512)} %get-tuple-element.1064) | copy-start | bytes 6148
  343.9 50.8 %copy-start.130 = (f32[2,512]{1,0:T(2,128)S(1)}, f32[2,512]{1,0:T(2,128)}, u32[]{:S(2)}) copy-start(f32[2,512]{1,0:T(2,128)} %copy-done.129) | copy-start | bytes 12292
  343.9 50.8 %copy-start.134 = (f32[2,512]{1,0:T(2,128)S(1)}, f32[2,512]{1,0:T(2,128)}, u32[]{:S(2)}) copy-start(f32[2,512]{1,0:T(2,128)} %copy-done.133) | copy-start | bytes 12292
  343.9 50.8 %copy-start.132 = (f32[2,512]{1,0:T(2,128)S(1)}, f32[2,512]{1,0:T(2,128)}, u32[]{:S(2)}) copy-start(f32[2,512]{1,0:T(2,128)} %copy-done.131) | copy-start | bytes 12292
  343.9 50.8 %copy-start.135 = (f32[2,512]{1,0:T(2,128)S(1)}, f32[2,512]{1,0:T(2,128)}, u32[]{:S(2)}) copy-start(f32[2,512]{1,0:T(2,128)} %get-tuple-element.1072) | copy-start | bytes 12292
  343.9 50.9 %copy-start.122 = (f32[2048]{0:T(1024)S(1)}, f32[2048]{0:T(1024)}, u32[]{:S(2)}) copy-start(f32[2048]{0:T(1024)} %copy-done.121) | copy-start | bytes 24580
  343.9 50.9 %copy-start.124 = (f32[2048]{0:T(1024)S(1)}, f32[2048]{0:T(1024)}, u32[]{:S(2)}) copy-start(f32[2048]{0:T(1024)} %copy-done.123) | copy-start | bytes 24580
  343.9 129.8 %copy-start.21 = (f32[1,512,512]{2,1,0:T(8,128)S(1)}, f32[1,512,512]{2,1,0:T(8,128)}, u32[]{:S(2)}) copy-start(f32[1,512,512]{2,1,0:T(8,128)} %copy-done.20) | copy-start | bytes 3145732
  753.6 4.9 copy-start.43
  762.1 4.4 copy-start.1
  (42 other events, 121.7 us)
Sparse Core Ops, SparseCore 0:
  337.2 416.2 all-reduce.6
where the time goes:
time: 787 us; the launch traced here: 774 us
  waiting for transfers between devices  295 us (37%)
  blocking collectives  126 us (16%)
  matrix products  120 us (15%)
  local copies, waits for them, and re-layouts  107 us (14%)
  other arithmetic  84 us (11%)
  loops' own time  19.8 us (3%)
  between operations  15.1 us (2%)
    psum x1, waiting for transfers between devices, body(): lax.psum((grads[0], grads[1], grads[2], grads[3], grads[4], grads[5], gra...  276 us
    psum x1, blocking collectives, body(): lax.psum((grads[0], grads[1], grads[2], grads[3], grads[4], grads[5], gra...  78.9 us
    psum x1, blocking collectives, body(): summed_shared = lax.psum((grads[8], grads[9], grads[10]), ('pipe', 'dp'))  47.1 us
    another operation x36, local copies, waits for them, and re-layouts  40 us
    dot_general x10, matrix products, product_left(): lax.dot_general(left, right, (((0,), (0,)), ((), ())), preferred_element_...  34.3 us
    dot_general x11, matrix products, product(): return jnp.dot(left, right, preferred_element_type=jnp.float32)  31.3 us
    dot_general x10, matrix products, product_right(): lax.dot_general(left, right, (((1,), (1,)), ((), ())), preferred_element_...  27.6 us
    cond x96, local copies, waits for them, and re-layouts  23.7 us
  transfers between devices with their start and end apart: 5, of which 2 were waited for; matrix products, arithmetic and copies ran while one was open for 20% of the time, Pallas kernels for 0%

commit v1 on v0

v1 whole, which is shorter than its diff:
```python
import functools
import math

import jax
import jax.numpy as jnp
from jax import lax
from jax.experimental import pallas as pl
from jax.experimental.pallas import tpu as pltpu
from jax.sharding import PartitionSpec as P

HEADS = 8
MESH = pl.DeviceIdType.MESH
norm_epsilon = 1e-05
masked_score = -1e30


def product(left, right):
    return jnp.dot(left, right, preferred_element_type=jnp.float32)


def product_left(left, right):
    return lax.dot_general(
        left, right, (((0,), (0,)), ((), ())), preferred_element_type=jnp.float32
    )


def product_right(left, right):
    return lax.dot_general(
        left, right, (((1,), (1,)), ((), ())), preferred_element_type=jnp.float32
    )


def gelu_both(values):
    cumulative = 0.5 * (1.0 + lax.erf(values * 0.7071067811865476))
    density = jnp.exp(-0.5 * values * values) * 0.3989422804014327
    return values * cumulative, cumulative + values * density


def norm_forward(values, gain_row, shift_row):
    centred = values - jnp.mean(values, axis=-1, keepdims=True)
    inverse = lax.rsqrt(jnp.mean(centred * centred, axis=-1, keepdims=True) + norm_epsilon)
    normed = centred * inverse
    return (normed * gain_row + shift_row, (normed, inverse))


def norm_backward(grad_out, saved_norm, gain_row):
    normed, inverse = saved_norm
    grad_normed = grad_out * gain_row
    grad_in = inverse * (
        grad_normed
        - jnp.mean(grad_normed, axis=-1, keepdims=True)
        - normed * jnp.mean(grad_normed * normed, axis=-1, keepdims=True)
    )
    return (grad_in, jnp.sum(grad_out * normed, axis=0), jnp.sum(grad_out, axis=0))


def attend_forward(queries, key_rows, value_rows, allowed):
    rows, features = queries.shape
    head_dim = features // HEADS
    split = lambda v: v.reshape(-1, HEADS, head_dim)
    scores = jnp.einsum(
        "qhd,khd->hqk", split(queries), split(key_rows), preferred_element_type=jnp.float32
    ) * head_dim ** (-0.5)
    scores = jnp.where(allowed[None], scores, masked_score)
    row_max = jnp.max(scores, axis=-1, keepdims=True)
    shifted = jnp.exp(scores - row_max)
    row_total = jnp.sum(shifted, axis=-1, keepdims=True)
    weights = (shifted / row_total).astype(jnp.bfloat16)
    mixed = jnp.einsum("hqk,khd->qhd", weights, split(value_rows), preferred_element_type=jnp.float32)
    return mixed.reshape(rows, features).astype(jnp.bfloat16), row_max + jnp.log(row_total)


def attend_backward(queries, key_rows, value_rows, allowed, log_totals, grad_mixed):
    rows, features = queries.shape
    head_dim = features // HEADS
    scale = head_dim ** (-0.5)
    split = lambda v: v.reshape(-1, HEADS, head_dim)
    q, k, v, g = map(split, (queries, key_rows, value_rows, grad_mixed))
    scores = jnp.einsum("qhd,khd->hqk", q, k, preferred_element_type=jnp.float32) * scale
    weights = jnp.where(allowed[None], jnp.exp(scores - log_totals), 0.0)
    grad_values = jnp.einsum(
        "hqk,qhd->khd", weights.astype(jnp.bfloat16), g, preferred_element_type=jnp.float32
    )
    grad_weights = jnp.einsum("qhd,khd->hqk", g, v, preferred_element_type=jnp.float32)
    centre = jnp.sum(weights * grad_weights, axis=-1, keepdims=True)
    grad_scores = (weights * (grad_weights - centre)).astype(jnp.bfloat16)
    grad_query = jnp.einsum("hqk,khd->qhd", grad_scores, k, preferred_element_type=jnp.float32) * scale
    grad_keys = jnp.einsum("hqk,qhd->khd", grad_scores, q, preferred_element_type=jnp.float32) * scale
    flat = lambda t: t.reshape(-1, features)
    return flat(grad_query), flat(grad_keys), flat(grad_values)


def attention_forward(rows_round, attn_block, allowed):
    n = rows_round.shape[1]
    packed = product(rows_round, attn_block[:, : 3 * n]).astype(jnp.bfloat16)
    mixed, logs = attend_forward(packed[:, :n], packed[:, n : 2 * n], packed[:, 2 * n :], allowed)
    return product(mixed, attn_block[:, 3 * n :]), (packed, mixed, logs)


def attention_backward(grad_added, rows_round, attn_block, allowed, kept):
    packed, mixed, logs = kept
    n = rows_round.shape[1]
    grad_round = grad_added.astype(jnp.bfloat16)
    grad_out_weight = product_left(mixed, grad_round)
    grad_mixed = product_right(grad_round, attn_block[:, 3 * n :]).astype(jnp.bfloat16)
    parts = attend_backward(
        packed[:, :n], packed[:, n : 2 * n], packed[:, 2 * n :], allowed, logs, grad_mixed
    )
    grad_packed = jnp.concatenate(parts, axis=1).astype(jnp.bfloat16)
    grad_in_weight = product_left(rows_round, grad_packed)
    grad_rows = product_right(grad_packed, attn_block[:, : 3 * n])
    return grad_rows, jnp.concatenate([grad_in_weight, grad_out_weight], axis=1)


def ffn_forward(hidden_round, ffn_first, bias_first, ffn_second, bias_second):
    inner = product(hidden_round, ffn_first) + bias_first
    active, slope = gelu_both(inner)
    active = active.astype(jnp.bfloat16)
    return product(active, ffn_second) + bias_second, (slope, active)


def ffn_backward(grad_branch, hidden_round, ffn_first, ffn_second, kept):
    slope, active = kept
    grad_round = grad_branch.astype(jnp.bfloat16)
    grad_second = product_left(active, grad_round)
    grad_bias_second = jnp.sum(grad_round.astype(jnp.float32), axis=0)
    grad_inner = (product_right(grad_round, ffn_second) * slope).astype(jnp.bfloat16)
    grad_first = product_left(hidden_round, grad_inner)
    grad_bias_first = jnp.sum(grad_inner.astype(jnp.float32), axis=0)
    grad_hidden = product_right(grad_inner, ffn_first)
    return grad_hidden, (grad_first, grad_bias_first, grad_second, grad_bias_second)


def halvings(rows, cols, count):
    sizes = [(rows, cols)]
    for _ in range(count):
        r, c = sizes[-1]
        sizes.append((r // 2, c) if r >= 32 else (r, c // 2))
    return sizes


def piece_list(shapes, count):
    chunks = []
    for t, (rows, cols) in enumerate(shapes):
        if rows <= 512 and cols > 1024:
            chunks += [(t, 0, c, rows, 1024) for c in range(0, cols, 1024)]
        elif rows > 1024:
            chunks += [(t, r, 0, 1024, cols) for r in range(0, rows, 1024)]
        else:
            chunks += [(t, 0, 0, rows, cols)]
    return chunks


def reduce_kernel(shapes, bits, g0, g1, g2, g3, small_ref, o0, o1, o2, o3, small_out,
                  r_sem, land0, land1, land2, land3, recv0, recv1, recv2, recv3,
                  small_acc, small_land, core_send, core_recv, send_sem, recv_sem,
                  small_send, small_recv):
    del r_sem
    grads = (g0, g1, g2, g3)
    total = (o0, o1, o2, o3)
    land = (land0, land1, land2, land3)
    arrive = (recv0, recv1, recv2, recv3)
    core = lax.axis_index("pipe")
    me = lax.axis_index("dp")
    orders = ([0, 2, 1, 3] + list(range(4, bits)), [1, 2, 0, 3] + list(range(4, bits)))
    orders = [[b for b in order if b < bits] for order in orders]
    my_bit = [lax.rem(me // (1 << b), 2) for b in range(bits)]
    partner = [
        {"dp": me + (1 << b) * (1 - 2 * my_bit[b])} for b in range(bits)
    ] + [{"pipe": 1 - core}]

    barrier = pltpu.get_barrier_semaphore()
    for device in partner:
        pl.semaphore_signal(barrier, inc=1, device_id=device, device_id_type=MESH)
    pl.semaphore_wait(barrier, len(partner))

    def remote(src, dst, send, recv, device):
        return pltpu.make_async_remote_copy(
            src_ref=src, dst_ref=dst, send_sem=send, recv_sem=recv,
            device_id=device, device_id_type=MESH,
        )

    chunks = piece_list(shapes, bits)

    small_acc[0] = small_ref[...]

    def small_copy(i):
        return remote(
            small_acc.at[i], small_land.at[i], small_send.at[i], small_recv.at[i], partner[i]
        )

    small_copy(0).start()

    def core_copy(k):
        t, r, c, rows, cols = chunks[k]
        where = (pl.ds(r, rows), pl.ds(c, cols))
        return remote(
            grads[t].at[(1 - core,) + where], arrive[t].at[where],
            core_send.at[k], core_recv.at[k], partner[bits],
        )

    def region(k, q, step):
        t, r, c, rows, cols = chunks[k]
        cols //= 2
        c = c + q * cols
        sizes = halvings(rows, cols, bits)
        for s in range(step):
            b = my_bit[orders[q][s]]
            (r0, c0), (r1, c1) = sizes[s], sizes[s + 1]
            if r1 != r0:
                r = r + b * r1
            else:
                c = c + b * c1
        return r, c, sizes[step]

    def other_region(k, q, step):
        r, c, (r0, c0) = region(k, q, step)
        t, _, _, rows, cols = chunks[k]
        r1, c1 = halvings(rows, cols // 2, bits)[step + 1]
        b = 1 - my_bit[orders[q][step]]
        if r1 != r0:
            r = r + b * r1
        else:
            c = c + b * c1
        return r, c, (r1, c1)

    def view(ref, reg):
        r, c, (rows, cols) = reg
        if not isinstance(r, int):
            r = pl.multiple_of(r, 16)
        if not isinstance(c, int):
            c = pl.multiple_of(c, 128)
        return ref.at[pl.ds(r, rows), pl.ds(c, cols)]

    def landing(k, q, step):
        t, r, c, rows, cols = chunks[k]
        cols //= 2
        c = c + q * cols
        sizes = halvings(rows, cols, bits)
        for s in range(step):
            (r0, c0), (r1, c1) = sizes[s], sizes[s + 1]
            if r1 != r0:
                r += r1
            else:
                c += c1
        return r, c, sizes[step + 1]

    def scatter_copy(k, q, step):
        t = chunks[k][0]
        return remote(
            view(arrive[t], other_region(k, q, step)), view(land[t], landing(k, q, step)),
            send_sem.at[k, q, step], recv_sem.at[k, q, step], partner[orders[q][step]],
        )

    def gather_copy(k, q, step):
        t = chunks[k][0]
        mine = region(k, q, step + 1)
        return remote(
            view(total[t], mine), view(total[t], mine),
            send_sem.at[k, q, 2 * bits - 1 - step], recv_sem.at[k, q, 2 * bits - 1 - step],
            partner[orders[q][step]],
        )

    def advance(k, stage):
        t, r, c, rows, cols = chunks[k]
        if stage == 0:
            core_copy(k).wait()
            where = (slice(r, r + rows), slice(c, c + cols))
            own = grads[t][(core,) + where].astype(jnp.float32)
            arrive[t][where] = (own + arrive[t][where].astype(jnp.float32)).astype(jnp.bfloat16)
        elif stage <= bits:
            for q in range(2):
                scatter_copy(k, q, stage - 1).wait()
                reg = region(k, q, stage)
                lr, lc, (lrows, lcols) = landing(k, q, stage - 1)
                mine = view(arrive[t], reg)
                into = view(total[t], reg) if stage == bits else mine
                got = land[t][lr : lr + lrows, lc : lc + lcols].astype(jnp.float32)
                into[...] = (mine[...].astype(jnp.float32) + got).astype(jnp.bfloat16)
        else:
            for q in range(2):
                gather_copy(k, q, 2 * bits - stage).wait()
        if stage < bits:
            for q in range(2):
                scatter_copy(k, q, stage).start()
        elif stage < 2 * bits:
            for q in range(2):
                gather_copy(k, q, 2 * bits - 1 - stage).start()

    for k in range(len(chunks)):
        core_copy(k).start()
    count, stages = len(chunks), 2 * bits + 1
    for t in range(count + stages - 1):
        for k in range(min(t, count - 1), -1, -1):
            if 0 <= t - k < stages:
                advance(k, t - k)
        if t <= bits:
            small_copy(t).wait()
            small_acc[t + 1] = small_acc[t] + small_land[t]
            if t < bits:
                small_copy(t + 1).start()
    small_out[...] = small_acc[bits + 1]


def reduce_all(grads, small, bits):
    shapes = tuple(g.shape[1:] for g in grads)
    vmem = pl.BlockSpec(memory_space=pltpu.VMEM)
    chunks = len(piece_list(shapes, bits))
    dma = pltpu.SemaphoreType.DMA
    return pl.pallas_call(
        functools.partial(reduce_kernel, shapes, bits),
        out_shape=[jax.ShapeDtypeStruct(s, jnp.bfloat16) for s in shapes]
        + [jax.ShapeDtypeStruct(small.shape, jnp.float32)],
        in_specs=[vmem] * 5,
        out_specs=[vmem] * 5,
        scratch_shapes=[pltpu.SemaphoreType.REGULAR]
        + [pltpu.VMEM(s, jnp.bfloat16) for s in shapes]
        + [pltpu.VMEM(s, jnp.bfloat16) for s in shapes]
        + [
            pltpu.VMEM((bits + 2,) + small.shape, jnp.float32),
            pltpu.VMEM((bits + 1,) + small.shape, jnp.float32),
            dma((chunks,)), dma((chunks,)),
            dma((chunks, 2, 2 * bits)), dma((chunks, 2, 2 * bits)),
            dma((bits + 1,)), dma((bits + 1,)),
        ],
        compiler_params=pltpu.CompilerParams(
            collective_id=0, has_side_effects=True, vmem_limit_bytes=56 << 20
        ),
    )(*grads, small)


def body(bits, inputs, src_len, tgt_len, groups, cotangent, attn_w, ffn_in, ffn_in_bias,
         ffn_out, ffn_out_bias, norm_gain, norm_bias, cross_w, cross_gain, cross_bias, pair_table):
    core = lax.axis_index("pipe")
    swap = lambda v: lax.ppermute(v, "pipe", [(0, 1), (1, 0)])
    first = core == 0

    def both(mine):
        other = swap(mine)
        return jnp.where(first, mine, other), jnp.where(first, other, mine)

    def both_pairs(mine):
        keep = lax.dynamic_index_in_dim(mine, core, 0, keepdims=False)
        other = swap(lax.dynamic_index_in_dim(mine, 1 - core, 0, keepdims=False))
        return jnp.where(first, keep, other), jnp.where(first, other, keep)

    f32 = lambda v: v.astype(jnp.float32)
    source, target = both_pairs(inputs[0])
    grad_memory_out, grad_target_out = both_pairs(cotangent[0])
    attn = both(attn_w[0])
    first_w = both(ffn_in[0])
    second_w = both(ffn_out[0])
    cross = both(cross_w)
    bias_first = both(f32(ffn_in_bias[0]))
    bias_second = both(f32(ffn_out_bias[0]))
    gains = both(f32(norm_gain[0]))
    shifts = both(f32(norm_bias[0]))
    cross_gain, cross_bias = f32(cross_gain), f32(cross_bias)

    pick = lambda v: lax.dynamic_index_in_dim(v, core, 0, keepdims=False)
    seq = inputs.shape[2]
    n = inputs.shape[3]
    positions = jnp.arange(seq, dtype=jnp.int32)
    source_live = positions < pick(src_len)
    target_live = positions < pick(tgt_len)
    hot = (pick(groups) == jnp.arange(pair_table.shape[0], dtype=jnp.int32)).astype(jnp.float32)
    tag = product(hot.astype(jnp.bfloat16)[None], pair_table)
    source_ok = jnp.broadcast_to(source_live[None], (seq, seq))
    target_ok = target_live[None] & (positions[None] <= positions[:, None])
    source_live = f32(source_live)[:, None]
    target_live = f32(target_live)[:, None]

    enc_in = f32(source) + tag
    enc_round = enc_in.astype(jnp.bfloat16)
    added, enc_attn = attention_forward(enc_round, attn[0], source_ok)
    h1e, saved_e1 = norm_forward(enc_in + added, gains[0][0], shifts[0][0])
    h1e_round = h1e.astype(jnp.bfloat16)
    branch, enc_ffn = ffn_forward(h1e_round, first_w[0], bias_first[0], second_w[0], bias_second[0])
    final, saved_e2 = norm_forward(enc_in + h1e + branch, gains[0][1], shifts[0][1])
    memory = final * source_live
    memory_round = memory.astype(jnp.bfloat16)
    memory_kv = product(memory_round, cross[0]).astype(jnp.bfloat16)
    dec_in = f32(target) + tag
    dec_round = dec_in.astype(jnp.bfloat16)
    added, dec_attn = attention_forward(dec_round, attn[1], target_ok)
    h1, saved_d1 = norm_forward(dec_in + added, gains[1][0], shifts[1][0])
    h1_round = h1.astype(jnp.bfloat16)
    cquery = product(h1_round, cross[1][:, :n]).astype(jnp.bfloat16)
    cmixed, clogs = attend_forward(cquery, memory_kv[:, :n], memory_kv[:, n:], source_ok)
    h2, saved_d2 = norm_forward(h1 + product(cmixed, cross[1][:, n:]), cross_gain, cross_bias)
    h2_round = h2.astype(jnp.bfloat16)
    branch, dec_ffn = ffn_forward(h2_round, first_w[1], bias_first[1], second_w[1], bias_second[1])
    final, saved_d3 = norm_forward(dec_in + h2 + branch, gains[1][1], shifts[1][1])
    decoded = final * target_live
    dsum, dg_d1, dc_d1 = norm_backward(f32(grad_target_out) * target_live, saved_d3, gains[1][1])
    dh, dec_f = ffn_backward(dsum, h2_round, first_w[1], second_w[1], dec_ffn)
    dpre2, dg_c, dc_c = norm_backward(dsum + dh, saved_d2, cross_gain)
    da = dpre2.astype(jnp.bfloat16)
    g_cross_out = product_left(cmixed, da)
    dcmixed = product_right(da, cross[1][:, n:]).astype(jnp.bfloat16)
    dq, dk, dv = attend_backward(cquery, memory_kv[:, :n], memory_kv[:, n:], source_ok, clogs, dcmixed)
    dcquery = dq.astype(jnp.bfloat16)
    dkv = jnp.concatenate([dk, dv], axis=1).astype(jnp.bfloat16)
    g_cross_q = product_left(h1_round, dcquery)
    dpre1, dg_d0, dc_d0 = norm_backward(dpre2 + product_right(dcquery, cross[1][:, :n]), saved_d1, gains[1][0])
    drows, g_attn_d = attention_backward(dpre1, dec_round, attn[1], target_ok, dec_attn)
    dtarget = dsum + dpre1 + drows
    g_cross_kv = product_left(memory_round, dkv)
    dmem = (f32(grad_memory_out) + product_right(dkv, cross[0])) * source_live
    dsum, dg_e1, dc_e1 = norm_backward(dmem, saved_e2, gains[0][1])
    dh, enc_f = ffn_backward(dsum, h1e_round, first_w[0], second_w[0], enc_ffn)
    dpre1, dg_e0, dc_e0 = norm_backward(dsum + dh, saved_e1, gains[0][0])
    drows, g_attn_e = attention_backward(dpre1, enc_round, attn[0], source_ok, enc_attn)
    dsource = dsum + dpre1 + drows

    low = lambda *vs: jnp.stack([v.astype(jnp.bfloat16) for v in vs])
    grads = (
        low(enc_f[2], dec_f[2]),
        low(enc_f[0], dec_f[0]),
        low(g_cross_kv, jnp.concatenate([g_cross_q, g_cross_out], axis=1)),
        low(g_attn_e, g_attn_d),
    )
    pair_grad = hot[:, None] * jnp.sum(dsource + dtarget, axis=0)[None]
    wide = lambda v: v.reshape(-1, n)
    section_rows = [
        jnp.concatenate([wide(f[1]), wide(f[3]), wide(g0), wide(g1), wide(c0), wide(c1)])
        for f, g0, g1, c0, c1 in (
            (enc_f, dg_e0, dg_e1, dc_e0, dc_e1), (dec_f, dg_d0, dg_d1, dc_d0, dc_d1)
        )
    ]
    small = jnp.concatenate(section_rows + [wide(dg_c), wide(dc_c), pair_grad])
    used = small.shape[0]
    small = jnp.pad(small, ((0, -used % 8), (0, 0)))
    out_g, first_g, cross_g, attn_g, small = reduce_all(grads, small, bits)

    per = section_rows[0].shape[0]
    mine = lax.dynamic_slice_in_dim(small, core * per, per, 0)
    ff = per - 5
    shared = small[2 * per :]

    def own(enc, dec):
        keep = jnp.where(first, enc, dec)
        other = swap(jnp.where(first, dec, enc))
        return jnp.where(first, jnp.stack([keep, other]), jnp.stack([other, keep]))[None]

    return (
        own(memory, decoded), own(dsource, dtarget),
        f32(attn_g)[None], f32(first_g)[None], mine[:ff].reshape(1, -1), f32(out_g)[None],
        mine[ff : ff + 1], mine[ff + 1 : ff + 3][None], mine[ff + 3 : ff + 5][None],
        f32(cross_g), shared[0], shared[1], shared[2 : 2 + pair_table.shape[0]],
    )


def solution(mesh):
    bits = int(math.log2(mesh.shape["dp"]))
    return jax.shard_map(
        functools.partial(body, bits),
        mesh=mesh,
        in_specs=(
            P("pipe", "dp", None, None), P("dp"), P("dp"), P("dp"), P("pipe", "dp", None, None),
            P("pipe", None, None), P("pipe", None, None), P("pipe", None), P("pipe", None, None),
            P("pipe", None), P("pipe", None, None), P("pipe", None, None), P(None, "pipe"),
            P(), P(), P(),
        ),
        out_specs=(
            P("pipe", "dp", None, None), P("pipe", "dp", None, None), P("pipe", None, None),
            P("pipe", None, None), P("pipe", None), P("pipe", None, None), P("pipe", None),
            P("pipe", None, None), P("pipe", None, None), P(None, "pipe"), P(), P(), P(),
        ),
        check_vma=False,
    )
```

time: 787 us -> 354 us (0.45)
  waiting for transfers between devices: 295 us -> 3.35 us
  Pallas kernels: 0 us -> 137 us
  blocking collectives: 126 us -> 0 us
  local copies, waits for them, and re-layouts: 107 us -> 30.8 us
  other arithmetic: 84 us -> 59.1 us
  loops' own time: 19.8 us -> 0 us
  between operations: 15.1 us -> 2.4 us
  matrix products: 120 us -> 112 us
    psum x1 -> x0, waiting for transfers between devices: 276 us -> none  [body(): lax.psum((grads[0], grads[1], grads[2], grads[3], grads[4], grads[5], gra...]
    pallas_call x0 -> x1, Pallas kernels: none -> 137 us  [reduce_all(): pl.pallas_call(functools.partial(reduce_kernel, shapes, bits), out_shape=...]
    psum x2 -> x0, blocking collectives: 126 us -> none  [the longest x1 78.9 us: body(): lax.psum((grads[0], grads[1], grads[2], grads[3], grads[4], grads[5], gra...]
    another operation x36 -> x0, local copies, waits for them, and re-layouts: 40 us -> none
    cond x102 -> x0, local copies, waits for them, and re-layouts: 38.9 us -> none
    broadcast_in_dim x5 -> x3, other arithmetic: 30.3 us -> 9.43 us  [the longest x1 4.28 us: body(): f32(attn_g)[None]]
    another operation x6 -> x0, loops' own time: 19.8 us -> none  [either(): return lax.cond(flag, work, nothing, operands)]
    ppermute x4 -> x12, waiting for transfers between devices: 18.4 us -> 3.35 us  [body(): swap = lambda v: lax.ppermute(v, 'pipe', [(0, 1), (1, 0)])]
  transfers between devices with their start and end apart: 5 -> 12, of which waited for: 2 -> 1; matrix products, arithmetic and copies ran while one was open for 20% -> 32% of each run, Pallas kernels for 0% -> 39%
where the time goes in v1:
time: 354 us; the launch traced here: 348 us
  Pallas kernels  137 us (39%)
  matrix products  112 us (32%)
  other arithmetic  59.1 us (17%)
  local copies, waits for them, and re-layouts  30.8 us (9%)
    pallas_call x1, Pallas kernels, reduce_all(): pl.pallas_call(functools.partial(reduce_kernel, shapes, bits), out_shape=...  137 us
    dot_general x11, matrix products, product_right(): lax.dot_general(left, right, (((1,), (1,)), ((), ())), preferred_element_...  24.7 us
    dot_general x11, matrix products, product_left(): lax.dot_general(left, right, (((0,), (0,)), ((), ())), preferred_element_...  23.9 us
    dot_general x12, matrix products, product(): return jnp.dot(left, right, preferred_element_type=jnp.float32)  22.8 us
    another operation x4, other arithmetic, body(): low = lambda *vs: jnp.stack([v.astype(jnp.bfloat16) for v in vs])  10.7 us
    unnamed x222, local copies, waits for them, and re-layouts  9.26 us
    dot_general x3, matrix products, attend_backward(): jnp.einsum('qhd,khd->hqk', g, v, preferred_element_type=jnp.float32)  8.74 us
    convert_element_type x3, other arithmetic, attend_backward(): grad_scores = (weights * (grad_weights - centre)).astype(jnp.bfloat16)  8.7 us
  transfers between devices with their start and end apart: 12, of which 1 were waited for; matrix products, arithmetic and copies ran while one was open for 32% of the time, Pallas kernels for 39%

profile of v1, /device:TPU:0, one launch (start us, length us, event | category | flops | bytes accessed | tf_op | source)
XLA Modules:
  0.0 347.7 jit_solution(2919504714460770831)
XLA Ops:
  12.3 1.7 constant_dynamic-slice_fusion.2
  20.8 3.3 collective-permute-done
  25.2 2.5 broadcast_select_fusion.6
  30.5 1.4 copy.78
  32.0 2.3 copy.77
  34.3 2.0 select_reduce_fusion.2
  36.4 2.2 fusion
  39.7 3.1 fusion.51
  44.6 2.0 fusion.153
  47.0 5.6 %multiply_convert_fusion.4 = (bf16[512,2048]{1,0:T(8,128)(2,1)S(1)}, f32[512,2048]{1,0:T(8,128)}) fusion(f32[2048]{0:T(1024)S(1)} %get-tuple-element.103, bf16[512,2048]{1,0:T(8,128)(2,1)} %collective-permute-done.4, pred[]{:T(512)S(6)} %eq.15, bf16[1,512,2048]{2,1,0:T(8,128)(2,1)} %param.22, f32[512,512]{0,1:T(8,128)S(1)} %get-tuple-element.121, ...), kind=kOutput, calls=%fused_computation.45 | convolution fusion | flops 1082392576 | bytes 11550721 | tf_op jit(solution)/shard_map/dot_general | solution.py:18
  52.7 1.5 fusion.154
  57.8 2.2 copy.86
  60.0 1.5 select_reduce_fusion.1
  61.5 2.2 fusion.1
  63.8 2.5 fusion.49
  66.3 1.7 fusion.155
  69.0 2.1 select_reduce_fusion
  71.1 2.0 fusion.2
  73.1 2.2 fusion.50
  76.9 3.7 %multiply_convert_fusion.3 = (bf16[512,2048]{1,0:T(8,128)(2,1)S(1)}, f32[512,2048]{1,0:T(8,128)S(1)}) fusion(f32[2048]{0:T(1024)S(1)} %get-tuple-element.102, bf16[512,2048]{1,0:T(8,128)(2,1)} %collective-permute-done.4, pred[]{:T(512)S(6)} %eq.15, bf16[1,512,2048]{2,1,0:T(8,128)(2,1)S(1)} %copy-done.100, f32[512,512]{0,1:T(8,128)S(1)} %get-tuple-element.133, ...), kind=kOutput, calls=%fused_computation.43 | convolution fusion | flops 1082392576 | bytes 11550721 | tf_op jit(solution)/shard_map/dot_general | solution.py:18
  80.7 3.2 fusion.157
  84.1 2.3 multiply_reduce_fusion.4
  86.4 2.1 convert_reduce_fusion.2
  88.5 2.7 fusion.31
  91.1 4.2 %convert_reduce_fusion = (f32[2048]{0:T(1024)S(1)}, bf16[512,2048]{1,0:T(8,128)(2,1)S(1)}) fusion(f32[512,2048]{1,0:T(8,128)S(1)} %get-tuple-element.135, f32[2048]{0:T(1024)S(1)} %copy-done.73, bf16[2048,512]{1,0:T(8,128)(2,1)} %collective-permute-done.6, pred[]{:T(512)S(6)} %eq.15, bf16[1,2048,512]{2,1,0:T(8,128)(2,1)S(1)} %copy-done.98, ...), kind=kOutput, calls=%fused_computation.41 | convolution fusion | flops 1088681984 | bytes 11550721 | tf_op jit(solution)/shard_map/dot_general | solution.py:28
  95.4 2.7 fusion.33
  98.0 3.8 %multiply_reduce_fusion.3 = (f32[512]{0:T(512)}, f32[512]{0:T(512)S(1)}, f32[512]{0:T(512)S(1)}, f32[512]{0:T(512)}, f32[512,512]{0,1:T(8,128)S(1)}) fusion(f32[512,512]{0,1:T(8,128)S(1)} %get-tuple-element.133, f32[512]{0:T(512)S(1)} %add_rsqrt_fusion.1, f32[512]{0:T(512)S(1)} %broadcast_multiply_fusion.12, f32[512]{0:T(512)S(1)} %copy-done.77, ...), kind=kOutput, calls=%fused_computation.135 | convolution fusion | flops 1077409792 | bytes 9451521 | tf_op jit(solution)/shard_map/dot_general | solution.py:28
  103.9 2.7 fusion.52
  106.5 2.9 multiply_reduce_fusion.2
  109.4 3.0 multiply_convert_fusion.2
  112.5 2.0 fusion.64
  114.5 1.4 fusion.61
  119.7 2.3 convolution_convert_fusion.10
  122.0 1.8 fusion.42
  125.5 2.7 fusion.30
  129.4 2.9 convert_reduce_fusion.1
  132.5 2.7 fusion.32
  135.2 1.6 multiply_reduce_fusion.7
  138.4 1.5 convolution_convert_fusion.11
  139.9 3.1 fusion.55
  143.0 2.9 multiply_reduce_fusion.1
  145.9 2.8 multiply_convert_fusion.1
  148.8 3.4 fusion.63
  152.2 1.6 fusion.62
  153.8 1.8 fusion.58
  155.7 3.0 multiply_reduce_fusion
  158.7 2.8 multiply_convert_fusion
  163.8 2.0 fusion.46
  165.7 2.2 fusion.35
  168.5 4.0 %fusion.34 = bf16[1,512,1536]{2,1,0:T(8,128)(2,1)} fusion(bf16[512,512]{0,1:T(8,128)(2,1)} %bitcast.347, bf16[512,512]{0,1:T(8,128)(2,1)} %bitcast.274, bf16[512,512]{0,1:T(8,128)(2,1)} %bitcast.276, bf16[512,512]{0,1:T(8,128)(2,1)} %copy-done.59, f32[512]{0:T(512)S(1)} %bitcast.338), kind=kOutput, calls=%fused_computation.68 | convolution fusion | flops 811597824 | bytes 3672064 | tf_op jit(solution)/shard_map/dot_general | solution.py:22
  172.5 3.9 %add_reduce_fusion = (f32[512]{0:T(512)S(1)}, f32[512,512]{0,1:T(8,128)}, f32[1,1,512,512]{2,3,1,0:T(8,128)}) fusion(f32[512,512]{0,1:T(8,128)} %fusion.46, pred[]{:T(512)S(6)} %eq.15, bf16[512,512]{0,1:T(8,128)(2,1)S(1)} %bitcast.348, bf16[512,512]{0,1:T(8,128)(2,1)S(1)} %bitcast.275, bf16[512,512]{0,1:T(8,128)(2,1)S(1)} %bitcast.277, ...), kind=kOutput, calls=%fused_computation.134 | convolution fusion | flops 811597312 | bytes 8390657 | tf_op jit(solution)/shard_map/dot_general | solution.py:28
  176.5 2.5 pad_maximum_fusion.g0
  180.2 2.4 pad_maximum_fusion.1.g1
  183.5 3.3 maximum_maximum_fusion.1.g2
  186.8 2.5 maximum_maximum_fusion.g3
  189.4 136.9 %shard_map.255 = (bf16[2048,512]{1,0:T(8,128)(2,1)}, bf16[512,2048]{1,0:T(8,128)(2,1)}, bf16[512,1024]{1,0:T(8,128)(2,1)}, bf16[512,2048]{1,0:T(8,128)(2,1)}, f32[32,512]{1,0:T(8,128)}) custom-call(bf16[2,2048,512]{2,1,0:T(8,128)(2,1)} %pad_maximum_fusion.g0, bf16[2,512,2048]{2,1,0:T(8,128)(2,1)} %pad_maximum_fusion.1.g1, ...), custom_call_target="tpu_custom_call" | custom-call | tf_op jit(solution)/shard_map/pallas_call | solution.py:310
  326.3 4.3 %bitcast_convert_fusion.2 = f32[1,512,2048]{2,1,0:T(8,128)} fusion(bf16[512,2048]{1,0:T(8,128)(2,1)} %get-tuple-element.18), kind=kLoop, calls=%fused_computation.75 | loop fusion | flops 1048576 | bytes 6291456 | tf_op jit(solution)/shard_map/broadcast_in_dim | solution.py:448
  330.6 2.5 bitcast_convert_fusion.1
  335.0 1.6 convert_element_type.331
  337.2 2.6 bitcast_convert_fusion
  339.8 2.0 maximum_select_fusion
  341.8 1.8 copy.111
  343.6 2.0 maximum_select_fusion.1
  345.6 1.8 copy.112
  (335 shorter events, 49.2 us)
Async XLA Ops:
  0.6 10.9 %copy-start = (bf16[8,512]{1,0:T(8,128)(2,1)S(1)}, bf16[8,512]{1,0:T(8,128)(2,1)}, u32[]{:S(2)}) copy-start(bf16[8,512]{1,0:T(8,128)(2,1)} %param.31) | copy-start | bytes 24580
  0.7 14.7 %copy-start.94 = (bf16[512]{0:T(512)(128)(2,1)S(1)}, bf16[512]{0:T(512)(128)(2,1)}, u32[]{:S(2)}) copy-start(bf16[512]{0:T(512)(128)(2,1)} %param.29) | copy-start | bytes 3076
  0.7 14.7 %copy-start.95 = (bf16[512]{0:T(512)(128)(2,1)S(1)}, bf16[512]{0:T(512)(128)(2,1)}, u32[]{:S(2)}) copy-start(bf16[512]{0:T(512)(128)(2,1)} %param.30) | copy-start | bytes 3076
  1.4 17.0 %collective-permute-start.7 = (f32[512]{0:T(512)S(1)}, f32[512]{0:T(512)S(1)}, u32[]{:S(2)}, u32[]{:S(2)}) collective-permute-start(f32[512]{0:T(512)S(1)} %bitcast.313), channel_id=1, source_target_pairs={{0,16},{16,0},{1,17},{17,1},{2,18},{18,2},{3,19},{19,3},{4,20},{20... | collective-permute-start | bytes 6152 | tf_op jit(solution)/shard_map/ppermute | solution.py:335
  2.5 16.6 %collective-permute-start.3 = (f32[2,512]{1,0:T(2,128)S(1)}, f32[2,512]{1,0:T(2,128)S(1)}, u32[]{:S(2)}, u32[]{:S(2)}) collective-permute-start(f32[2,512]{1,0:T(2,128)S(1)} %bitcast_convert_fusion.3), channel_id=1, source_target_pairs={{0,16},{16,0},{1,17},{17,1},{2,18},{18,2},{3,19},{19,3},{4,20},{20... | collective-permute-start | bytes 12296 | tf_op jit(solution)/shard_map/ppermute | solution.py:335
  3.3 16.3 %collective-permute-start.2 = (f32[2,512]{1,0:T(2,128)S(1)}, f32[2,512]{1,0:T(2,128)S(1)}, u32[]{:S(2)}, u32[]{:S(2)}) collective-permute-start(f32[2,512]{1,0:T(2,128)S(1)} %bitcast_convert_fusion.4), channel_id=1, source_target_pairs={{0,16},{16,0},{1,17},{17,1},{2,18},{18,2},{3,19},{19,3},{4,20},{20... | collective-permute-start | bytes 12296 | tf_op jit(solution)/shard_map/ppermute | solution.py:335
  4.4 15.9 %collective-permute-start.5 = (f32[2048]{0:T(1024)S(1)}, f32[2048]{0:T(1024)S(1)}, u32[]{:S(2)}, u32[]{:S(2)}) collective-permute-start(f32[2048]{0:T(1024)S(1)} %bitcast.291), channel_id=1, source_target_pairs={{0,16},{16,0},{1,17},{17,1},{2,18},{18,2},{3,19},{19,3},{4,20},{20... | collective-permute-start | bytes 24584 | tf_op jit(solution)/shard_map/ppermute | solution.py:335
  4.5 20.6 %collective-permute-start.8 = (bf16[512,1024]{1,0:T(8,128)(2,1)}, bf16[512,1024]{1,0:T(8,128)(2,1)}, u32[]{:S(2)}, u32[]{:S(2)}) collective-permute-start(bf16[512,1024]{1,0:T(8,128)(2,1)} %param.28), channel_id=1, source_target_pairs={{0,16},{16,0},{1,17},{17,1},{2,18},{18,2},{3,19},{19,3},{4,20},{20... | collective-permute-start | bytes 3145736 | tf_op jit(solution)/shard_map/ppermute | solution.py:335
  11.5 52.2 %copy-start.9 = (pred[512,512]{0,1:T(8,128)(4,1)}, pred[512,512]{0,1:T(8,128)(4,1)S(1)}, u32[]{:S(2)}) copy-start(pred[512,512]{0,1:T(8,128)(4,1)S(1)} %fusion.76) | copy-start | bytes 786436
  12.3 32.3 %copy-start.87 = (f32[1,512]{1,0:T(1,128)}, f32[1,512]{1,0:T(1,128)S(1)}, u32[]{:S(2)}) copy-start(f32[1,512]{1,0:T(1,128)S(1)} %fusion.104) | copy-start | bytes 6148
  12.3 7.3 %copy-start.70 = (bf16[1,2,512]{2,1,0:T(2,128)(2,1)S(1)}, bf16[1,2,512]{2,1,0:T(2,128)(2,1)}, u32[]{:S(2)}) copy-start(bf16[1,2,512]{2,1,0:T(2,128)(2,1)} %param.27) | copy-start | bytes 6148
  12.3 7.3 %copy-start.71 = (bf16[1,2,512]{2,1,0:T(2,128)(2,1)S(1)}, bf16[1,2,512]{2,1,0:T(2,128)(2,1)}, u32[]{:S(2)}) copy-start(bf16[1,2,512]{2,1,0:T(2,128)(2,1)} %param.26) | copy-start | bytes 6148
  14.0 11.1 %copy-start.52 = (bf16[512,1024]{1,0:T(8,128)(2,1)S(1)}, bf16[512,1024]{1,0:T(8,128)(2,1)}, u32[]{:S(2)}) copy-start(bf16[512,1024]{1,0:T(8,128)(2,1)} %param.28) | copy-start | bytes 3145732
  15.3 65.3 %copy-start.76 = (f32[512]{0:T(512)}, f32[512]{0:T(512)S(1)}, u32[]{:S(2)}) copy-start(f32[512]{0:T(512)S(1)} %convert_element_type.296) | copy-start | bytes 6148
  18.4 9.3 %copy-start.42 = (bf16[1,512,2048]{2,1,0:T(8,128)(2,1)S(1)}, bf16[1,512,2048]{2,1,0:T(8,128)(2,1)}, u32[]{:S(2)}) copy-start(bf16[1,512,2048]{2,1,0:T(8,128)(2,1)} %param.21) | copy-start | bytes 6291460
  18.4 9.3 %collective-permute-start.1 = (bf16[512,2048]{1,0:T(8,128)(2,1)}, bf16[512,2048]{1,0:T(8,128)(2,1)S(1)}, u32[]{:S(2)}, u32[]{:S(2)}) collective-permute-start(bf16[512,2048]{1,0:T(8,128)(2,1)} %bitcast.273), channel_id=1, source_target_pairs={{0,16},{16,0},{1,17},{17,1},{2,18},{18,2},{3,19},{19,3},{4,20},{20... | collective-permute-start | bytes 6291464 | tf_op jit(solution)/shard_map/ppermute | solution.py:335
  19.1 5.0 %collective-permute-start = (bf16[512,512]{0,1:T(8,128)(2,1)S(1)}, bf16[512,512]{0,1:T(8,128)(2,1)S(1)}, u32[]{:S(2)}, u32[]{:S(2)}) collective-permute-start(bf16[512,512]{0,1:T(8,128)(2,1)S(1)} %bitcast.284), channel_id=1, source_target_pairs={{0,16},{16,0},{1,17},{17,1},{2,18},{18,2},{3,19},{19,3},{4,20},{20... | collective-permute-start | bytes 1572872 | tf_op jit(solution)/shard_map/ppermute | solution.py:335
  19.6 64.5 %collective-permute-start.10 = (bf16[512,512]{0,1:T(8,128)(2,1)}, bf16[512,512]{0,1:T(8,128)(2,1)}, u32[]{:S(2)}, u32[]{:S(2)}) collective-permute-start(bf16[512,512]{0,1:T(8,128)(2,1)} %bitcast.42), channel_id=1, source_target_pairs={{0,16},{16,0},{1,17},{17,1},{2,18},{18,2},{3,19},{19,3},{4,20},{20... | collective-permute-start | bytes 1572872 | tf_op jit(solution)/shard_map/ppermute | solution.py:335
  20.2 32.4 %copy-start.90 = (f32[1,512]{1,0:T(1,128)}, f32[1,512]{1,0:T(1,128)S(1)}, u32[]{:S(2)}) copy-start(f32[1,512]{1,0:T(1,128)S(1)} %get-tuple-element.117) | copy-start | bytes 6148
  20.3 32.4 %copy-start.80 = (f32[1,512]{1,0:T(1,128)}, f32[1,512]{1,0:T(1,128)S(1)}, u32[]{:S(2)}) copy-start(f32[1,512]{1,0:T(1,128)S(1)} %get-tuple-element.115) | copy-start | bytes 6148
  20.3 32.3 %collective-permute-start.6 = (bf16[2048,512]{1,0:T(8,128)(2,1)}, bf16[2048,512]{1,0:T(8,128)(2,1)}, u32[]{:S(2)}, u32[]{:S(2)}) collective-permute-start(bf16[2048,512]{1,0:T(8,128)(2,1)} %bitcast.345), channel_id=1, source_target_pairs={{0,16},{16,0},{1,17},{17,1},{2,18},{18,2},{3,19},{19,3},{4,20},{20... | collective-permute-start | bytes 6291464 | tf_op jit(solution)/shard_map/ppermute | solution.py:335
  20.8 55.3 %copy-start.72 = (f32[2048]{0:T(1024)}, f32[2048]{0:T(1024)S(1)}, u32[]{:S(2)}) copy-start(f32[2048]{0:T(1024)S(1)} %get-tuple-element.102) | copy-start | bytes 24580
  24.1 22.8 %collective-permute-start.4 = (bf16[512,2048]{1,0:T(8,128)(2,1)}, bf16[512,2048]{1,0:T(8,128)(2,1)}, u32[]{:S(2)}, u32[]{:S(2)}) collective-permute-start(bf16[512,2048]{1,0:T(8,128)(2,1)} %bitcast.346), channel_id=1, source_target_pairs={{0,16},{16,0},{1,17},{17,1},{2,18},{18,2},{3,19},{19,3},{4,20},{20... | collective-permute-start | bytes 6291464 | tf_op jit(solution)/shard_map/ppermute | solution.py:335
  28.0 14.7 %copy-start.26 = (bf16[512,2048]{1,0:T(8,128)(2,1)}, bf16[512,2048]{1,0:T(8,128)(2,1)S(1)}, u32[]{:S(2)}) copy-start(bf16[512,2048]{1,0:T(8,128)(2,1)S(1)} %get-tuple-element.74) | copy-start | bytes 6291460
  30.5 5.8 %copy-start.11 = (bf16[512,512]{0,1:T(8,128)(2,1)}, bf16[512,512]{0,1:T(8,128)(2,1)S(1)}, u32[]{:S(2)}) copy-start(bf16[512,512]{0,1:T(8,128)(2,1)S(1)} %copy.79) | copy-start | bytes 1572868
  32.0 10.7 %copy-start.15 = (bf16[512,512]{0,1:T(8,128)(2,1)}, bf16[512,512]{0,1:T(8,128)(2,1)S(1)}, u32[]{:S(2)}) copy-start(bf16[512,512]{0,1:T(8,128)(2,1)S(1)} %copy.78) | copy-start | bytes 1572868
  44.2 15.9 %copy-start.13 = (bf16[512,512]{0,1:T(8,128)(2,1)}, bf16[512,512]{0,1:T(8,128)(2,1)S(1)}, u32[]{:S(2)}) copy-start(bf16[512,512]{0,1:T(8,128)(2,1)S(1)} %copy.84) | copy-start | bytes 1572868
  44.4 15.6 %copy-start.16 = (bf16[512,512]{0,1:T(8,128)(2,1)}, bf16[512,512]{0,1:T(8,128)(2,1)S(1)}, u32[]{:S(2)}) copy-start(bf16[512,512]{0,1:T(8,128)(2,1)S(1)} %copy.83) | copy-start | bytes 1572868
  44.6 19.1 %copy-start.34 = (bf16[512,512]{0,1:T(8,128)(2,1)}, bf16[512,512]{0,1:T(8,128)(2,1)S(1)}, u32[]{:S(2)}) copy-start(bf16[512,512]{0,1:T(8,128)(2,1)S(1)} %copy.82) | copy-start | bytes 1572868
  46.7 5.9 %copy-start.22 = (f32[512,512]{0,1:T(8,128)}, f32[512,512]{0,1:T(8,128)S(1)}, u32[]{:S(2)}) copy-start(f32[512,512]{0,1:T(8,128)S(1)} %get-tuple-element.121) | copy-start | bytes 3145732
  46.9 5.7 %copy-start.78 = (f32[512]{0:T(512)}, f32[512]{0:T(512)S(1)}, u32[]{:S(2)}) copy-start(f32[512]{0:T(512)S(1)} %add_rsqrt_fusion.4) | copy-start | bytes 6148
  46.9 5.7 %copy-start.60 = (bf16[512,512]{0,1:T(8,128)(2,1)S(1)}, bf16[512,512]{0,1:T(8,128)(2,1)}, u32[]{:S(2)}) copy-start(bf16[512,512]{0,1:T(8,128)(2,1)} %copy-done.59) | copy-start | bytes 1572868
  46.9 5.7 %copy-start.85 = (f32[512]{0:T(512)S(1)}, f32[512]{0:T(512)}, u32[]{:S(2)}) copy-start(f32[512]{0:T(512)} %get-tuple-element.113) | copy-start | bytes 6148
  46.9 5.7 %copy-start.88 = (f32[1,512]{1,0:T(1,128)S(1)}, f32[1,512]{1,0:T(1,128)}, u32[]{:S(2)}) copy-start(f32[1,512]{1,0:T(1,128)} %copy-done.87) | copy-start | bytes 6148
  47.0 5.7 %copy-start.97 = (bf16[1,2048,512]{2,1,0:T(8,128)(2,1)S(1)}, bf16[1,2048,512]{2,1,0:T(8,128)(2,1)}, u32[]{:S(2)}) copy-start(bf16[1,2048,512]{2,1,0:T(8,128)(2,1)} %param.24) | copy-start | bytes 6291460
  54.2 32.2 %copy-start.5 = (f32[512,512]{0,1:T(8,128)}, f32[512,512]{0,1:T(8,128)S(1)}, u32[]{:S(2)}) copy-start(f32[512,512]{0,1:T(8,128)S(1)} %get-tuple-element.125) | copy-start | bytes 3145732
  57.8 11.2 %copy-start.18 = (bf16[512,512]{0,1:T(8,128)(2,1)}, bf16[512,512]{0,1:T(8,128)(2,1)S(1)}, u32[]{:S(2)}) copy-start(bf16[512,512]{0,1:T(8,128)(2,1)S(1)} %copy.87) | copy-start | bytes 1572868
  63.7 4.5 %copy-start.20 = (bf16[512,1024]{1,0:T(8,128)(2,1)S(1)}, bf16[512,1024]{1,0:T(8,128)(2,1)}, u32[]{:S(2)}) copy-start(bf16[512,1024]{1,0:T(8,128)(2,1)} %broadcast_select_fusion.6) | copy-start | bytes 3145732
  63.8 4.5 %copy-start.92 = (f32[1,512]{1,0:T(1,128)S(1)}, f32[1,512]{1,0:T(1,128)}, u32[]{:S(2)}) copy-start(f32[1,512]{1,0:T(1,128)} %get-tuple-element.111) | copy-start | bytes 6148
  66.3 4.7 %copy-start.67 = (bf16[8,64,512]{2,1,0:T(8,128)(2,1)}, bf16[8,64,512]{2,1,0:T(8,128)(2,1)S(1)}, u32[]{:S(2)}) copy-start(bf16[8,64,512]{2,1,0:T(8,128)(2,1)S(1)} %fusion.49) | copy-start | bytes 1572868
  68.0 7.3 %copy-start.3 = (f32[512,512]{0,1:T(8,128)}, f32[512,512]{0,1:T(8,128)S(1)}, u32[]{:S(2)}) copy-start(f32[512,512]{0,1:T(8,128)S(1)} %get-tuple-element.129) | copy-start | bytes 3145732
  88.5 9.6 %copy-start.57 = (f32[512,512]{0,1:T(8,128)}, f32[512,512]{0,1:T(8,128)S(1)}, u32[]{:S(2)}) copy-start(f32[512,512]{0,1:T(8,128)S(1)} %get-tuple-element.70) | copy-start | bytes 3145732
  91.1 4.2 %copy-start.77 = (f32[512]{0:T(512)S(1)}, f32[512]{0:T(512)}, u32[]{:S(2)}) copy-start(f32[512]{0:T(512)} %copy-done.76) | copy-start | bytes 6148
  118.4 5.4 %copy-start.41 = (bf16[1,1,512,512]{2,3,1,0:T(8,128)(2,1)S(1)}, bf16[1,1,512,512]{2,3,1,0:T(8,128)(2,1)}, u32[]{:S(2)}) copy-start(bf16[1,1,512,512]{2,3,1,0:T(8,128)(2,1)} %copy.90) | copy-start | bytes 1572868
  118.4 5.4 %copy-start.54 = (bf16[512,1024]{1,0:T(8,128)(2,1)S(1)}, bf16[512,1024]{1,0:T(8,128)(2,1)}, u32[]{:S(2)}) copy-start(bf16[512,1024]{1,0:T(8,128)(2,1)} %param.28) | copy-start | bytes 3145732
  125.5 9.7 %copy-start.55 = (f32[512,512]{0,1:T(8,128)}, f32[512,512]{0,1:T(8,128)S(1)}, u32[]{:S(2)}) copy-start(f32[512,512]{0,1:T(8,128)S(1)} %get-tuple-element.72) | copy-start | bytes 3145732
  132.4 7.4 %slice-start = ((s8[8388608]{0:T(1024)(128)(4,1)}), s8[4194304]{0:T(1024)(128)(4,1)S(1)}, s32[]{:S(2)}) async-start(s8[8388608]{0:T(1024)(128)(4,1)} %bitcast.245), calls=%async_computation | async-start | bytes 8388608
  135.1 4.8 %slice-start.1 = ((s8[8388608]{0:T(1024)(128)(4,1)}), s8[4194304]{0:T(1024)(128)(4,1)S(1)}, s32[]{:S(2)}) async-start(s8[8388608]{0:T(1024)(128)(4,1)} %bitcast.245), calls=%async_computation.1 | async-start | bytes 8388608
  137.1 5.9 %copy-start.7 = (f32[512,512]{0,1:T(8,128)}, f32[512,512]{0,1:T(8,128)S(1)}, u32[]{:S(2)}) copy-start(f32[512,512]{0,1:T(8,128)S(1)} %subtract_multiply_fusion.1) | copy-start | bytes 3145732
  148.7 5.1 %copy-start.10 = (pred[512,512]{0,1:T(8,128)(4,1)S(1)}, pred[512,512]{0,1:T(8,128)(4,1)}, u32[]{:S(2)}) copy-start(pred[512,512]{0,1:T(8,128)(4,1)} %copy-done.9) | copy-start | bytes 786436
  148.8 5.0 %copy-start.39 = (bf16[512,512]{0,1:T(8,128)(2,1)S(1)}, bf16[512,512]{0,1:T(8,128)(2,1)}, u32[]{:S(2)}) copy-start(bf16[512,512]{0,1:T(8,128)(2,1)} %convolution_convert_fusion.10) | copy-start | bytes 1572868
  167.9 4.6 %copy-start.8 = (f32[512,512]{0,1:T(8,128)S(1)}, f32[512,512]{0,1:T(8,128)}, u32[]{:S(2)}) copy-start(f32[512,512]{0,1:T(8,128)} %copy-done.7) | copy-start | bytes 3145732
  167.9 4.6 %copy-start.25 = (bf16[512,2048]{1,0:T(8,128)(2,1)S(1)}, bf16[512,2048]{1,0:T(8,128)(2,1)}, u32[]{:S(2)}) copy-start(bf16[512,2048]{1,0:T(8,128)(2,1)} %copy-done.24) | copy-start | bytes 6291460
  167.9 171.8 %collective-permute-start.9 = (f32[512,512]{0,1:T(8,128)}, f32[512,512]{0,1:T(8,128)}, u32[]{:S(2)}, u32[]{:S(2)}) collective-permute-start(f32[512,512]{0,1:T(8,128)} %get-tuple-element.87), channel_id=1, source_target_pairs={{0,16},{16,0},{1,17},{17,1},{2,18},{18,2},{3,19},{19,3},{4,20},{20... | collective-permute-start | bytes 3145736 | tf_op jit(solution)/shard_map/ppermute | solution.py:335
  168.5 4.1 %copy-start.65 = (bf16[8,64,512]{2,1,0:T(8,128)(2,1)S(1)}, bf16[8,64,512]{2,1,0:T(8,128)(2,1)}, u32[]{:S(2)}) copy-start(bf16[8,64,512]{2,1,0:T(8,128)(2,1)} %fusion.62) | copy-start | bytes 1572868
  168.5 4.1 %copy-start.102 = (bf16[8,64,512]{2,1,0:T(8,128)(2,1)S(1)}, bf16[8,64,512]{2,1,0:T(8,128)(2,1)}, u32[]{:S(2)}) copy-start(bf16[8,64,512]{2,1,0:T(8,128)(2,1)} %fusion.55) | copy-start | bytes 1572868
  176.4 167.1 %collective-permute-start.11 = (f32[512,512]{0,1:T(8,128)}, f32[512,512]{0,1:T(8,128)}, u32[]{:S(2)}, u32[]{:S(2)}) collective-permute-start(f32[512,512]{0,1:T(8,128)} %get-tuple-element.79), channel_id=1, source_target_pairs={{0,16},{16,0},{1,17},{17,1},{2,18},{18,2},{3,19},{19,3},{4,20},{20... | collective-permute-start | bytes 3145736 | tf_op jit(solution)/shard_map/ppermute | solution.py:335
  182.6 4.2 %copy-start.37 = (bf16[1,512,512]{2,1,0:T(8,128)(2,1)S(1)}, bf16[1,512,512]{2,1,0:T(8,128)(2,1)}, u32[]{:S(2)}) copy-start(bf16[1,512,512]{2,1,0:T(8,128)(2,1)} %fusion.70) | copy-start | bytes 1572868
  182.6 4.2 %copy-start.38 = (bf16[1,512,512]{2,1,0:T(8,128)(2,1)S(1)}, bf16[1,512,512]{2,1,0:T(8,128)(2,1)}, u32[]{:S(2)}) copy-start(bf16[1,512,512]{2,1,0:T(8,128)(2,1)} %fusion.69) | copy-start | bytes 1572868
  182.6 4.2 %copy-start.48 = (bf16[1,512,1536]{2,1,0:T(8,128)(2,1)S(1)}, bf16[1,512,1536]{2,1,0:T(8,128)(2,1)}, u32[]{:S(2)}) copy-start(bf16[1,512,1536]{2,1,0:T(8,128)(2,1)} %fusion.35) | copy-start | bytes 4718596
  326.3 4.3 %copy-start.29 = (bf16[512,2048]{1,0:T(8,128)(2,1)S(1)}, bf16[512,2048]{1,0:T(8,128)(2,1)}, u32[]{:S(2)}) copy-start(bf16[512,2048]{1,0:T(8,128)(2,1)} %get-tuple-element.19) | copy-start | bytes 6291460
  330.6 4.4 %copy-start.51 = (bf16[512,1024]{1,0:T(8,128)(2,1)S(1)}, bf16[512,1024]{1,0:T(8,128)(2,1)}, u32[]{:S(2)}) copy-start(bf16[512,1024]{1,0:T(8,128)(2,1)} %get-tuple-element.22) | copy-start | bytes 3145732
  330.6 6.6 %copy-start.28 = (bf16[2048,512]{1,0:T(8,128)(2,1)S(1)}, bf16[2048,512]{1,0:T(8,128)(2,1)}, u32[]{:S(2)}) copy-start(bf16[2048,512]{1,0:T(8,128)(2,1)} %get-tuple-element.21) | copy-start | bytes 6291460
  335.0 4.8 %copy-start.19 = (f32[1,1,512,512]{2,3,1,0:T(8,128)S(1)}, f32[1,1,512,512]{2,3,1,0:T(8,128)}, u32[]{:S(2)}) copy-start(f32[1,1,512,512]{2,3,1,0:T(8,128)} %get-tuple-element.88) | copy-start | bytes 3145732
  (57 other events, 160.3 us)
